TPU v7x, 32 devices: a whole 2x2x4 slice. The times are simulated.
32 devices in a mesh: grp: 2 (over x), tile: 16 (over z, y, core).
Axes of the slice: x: 2, y: 2, z: 4, core: 2. Of those that a mesh axis runs over, the one named last changes fastest.
Arguments:
- full_resolution_frames: bfloat16 [32, 2, 512, 512], P(('grp', 'tile')), parts along dimension 0, may hold values from -24 to 24
- height_angle_factor: float32 [1024, 512], P('grp'), parts along dimension 0, may hold values from -4 to 4
- normal_spacings: float32 [32], P('grp'), parts along dimension 0, may hold values from -2 to 2
- couple_entry_flags: int32 [16, 3], replicated, may hold values from 0 to 1, as said below
- block_target_indices: int32 [32, 64], P('grp'), parts along dimension 0, may hold values from 0 to 255, as said below
- block_target_totals: int32 [32], P('grp'), parts along dimension 0, may hold values from 1 to 64, as said below
Outputs:
- coherence: float32 [32, 3, 128, 32], P(('grp', 'tile')), parts along dimension 0
- velocities: float32 [2048, 15], P(('grp', 'tile')), parts along dimension 0
There are 2 independent parts, one for each index of `grp`. A program takes and returns all parts, laid end to end along the dimension named above; an argument that names none is the same for every part. Nothing has to cross between parts.
Inputs may be any that keep to these rules, and one draw needn't show every extreme that they name: `couple_entry_flags`: slot k-1 of date d stands for the pair of d and d + k; slot 0 is 1 wherever d + 1 < 16; slots with d + k >= 16 are 0. `block_target_indices`: row t lists distinct looked pixels of tile t; entries at or past the tile's count are 0. `block_target_totals`: some tile has exactly 64.
All inputs are finite; a program needn't handle non-finite values.
Results may differ from a plain program's by a relative error of at most 0.0003.
Values may be sent and summed in bfloat16 or wider, within the bound.
A program may use at most 192 MiB of HBM per device.

v0:
```python
import jax
import jax.numpy as jnp
from jax import lax
from jax.sharding import PartitionSpec as P

LOOK_ROWS = 4
LOOK_COLS = 16


EPSILON = 1e-06


def from_behind(block, axis, distance):
    devices = range(lax.axis_size(axis))
    route = [(i - distance, i) for i in devices if i - distance in devices]
    return lax.ppermute(block, axis, route)


def pooling_matrix(cols):
    column_index = jnp.arange(cols, dtype=jnp.int32)[:, None]
    look_index = jnp.arange(cols // LOOK_COLS, dtype=jnp.int32)[None, :]
    member = (column_index // LOOK_COLS == look_index).astype(jnp.float32)
    return member * (1.0 / (LOOK_ROWS * LOOK_COLS))


def looked(field, pooling):
    rows = field.shape[-2]
    cols = field.shape[-1]
    row_sums = jnp.sum(
        field.reshape(field.shape[:-2] + (rows // LOOK_ROWS, LOOK_ROWS, cols)), axis=-2
    )
    return jnp.einsum("...c,cl->...l", row_sums, pooling, precision=lax.Precision.HIGHEST)


def own_power(own_real, own_imag, pooling):
    return looked(own_real * own_real + own_imag * own_imag, pooling)


def pair_stats(own_real, own_imag, power_own, other_real, other_imag, theta, pooling):
    cross_real = own_real * other_real + own_imag * other_imag
    cross_imag = own_imag * other_real - own_real * other_imag
    cosine = jnp.cos(theta)
    sine = jnp.sin(theta)
    flat_real = cross_real * cosine + cross_imag * sine
    flat_imag = cross_imag * cosine - cross_real * sine
    other_energy = other_real * other_real + other_imag * other_imag
    means = looked(jnp.stack([flat_real, flat_imag, other_energy], axis=0), pooling)
    mean_real = means[0]
    mean_imag = means[1]
    power_other = means[2]
    scale = 1.0 / jnp.sqrt(power_own * power_other + EPSILON)
    return (jnp.sqrt(mean_real * mean_real + mean_imag * mean_imag) * scale, mean_imag * scale)


def inverse_map(couple_entry_flags):
    dates = couple_entry_flags.shape[0]
    later_mates = couple_entry_flags.shape[1]
    count = dates * later_mates
    pair_index = jnp.arange(count, dtype=jnp.int32)
    first_date = pair_index // later_mates
    pair_span = pair_index % later_mates + 1
    interval_index = jnp.arange(dates - 1, dtype=jnp.int32)
    covered = (interval_index[None, :] >= first_date[:, None]) & (
        interval_index[None, :] < (first_date + pair_span)[:, None]
    )
    design = couple_entry_flags.reshape(count).astype(jnp.float32)[:, None] * covered.astype(
        jnp.float32
    )
    normal = jnp.dot(design.T, design, precision=lax.Precision.HIGHEST)
    factor = jnp.linalg.cholesky(normal)
    partial_solve = lax.linalg.triangular_solve(factor, design.T, left_side=True, lower=True)
    return lax.linalg.triangular_solve(
        factor, partial_solve, left_side=True, lower=True, transpose_a=True
    )


def local(
    full_resolution_frames,
    height_angle_factor,
    normal_spacings,
    couple_entry_flags,
    block_target_indices,
    block_target_totals,
):
    tile_count = lax.axis_size("tile")
    entry_location = lax.axis_index("tile")
    dates = couple_entry_flags.shape[0]
    later_mates = couple_entry_flags.shape[1]
    image_rows = height_angle_factor.shape[0]
    image_cols = height_angle_factor.shape[1]
    tile_rows = image_rows // tile_count
    looked_cols = image_cols // LOOK_COLS
    tile_pix = tile_rows // LOOK_ROWS * looked_cols
    slot_count = block_target_indices.shape[1]
    pooling = pooling_matrix(image_cols)
    slots = lax.dynamic_index_in_dim(block_target_indices, entry_location, 0, keepdims=False)
    spacing_extended = jnp.concatenate(
        [normal_spacings, jnp.zeros((later_mates,), normal_spacings.dtype)], axis=0
    )
    own = full_resolution_frames[0].astype(jnp.float32)
    power_own = own_power(own[0], own[1], pooling)
    reference_spacing = lax.dynamic_index_in_dim(normal_spacings, entry_location, 0, keepdims=False)
    cohs = []
    phases = []
    for offset in range(1, later_mates + 1):
        other = from_behind(full_resolution_frames, "tile", -offset)[0].astype(jnp.float32)
        other_base = lax.dynamic_index_in_dim(
            spacing_extended, entry_location + offset, 0, keepdims=False
        )
        theta = (reference_spacing - other_base) * height_angle_factor
        coh, phase = pair_stats(own[0], own[1], power_own, other[0], other[1], theta, pooling)
        cohs.append(coh)
        phases.append(phase)
    coh_stack = jnp.stack(cohs, axis=0)
    phase_stack = jnp.stack(phases, axis=0)
    mask_row = lax.dynamic_slice_in_dim(couple_entry_flags, entry_location, 1, 0).astype(
        jnp.float32
    )
    coherence = coh_stack[None] * mask_row[:, :, None, None]
    phase_local = phase_stack[None]
    arrived = lax.all_to_all(phase_local, "tile", split_axis=2, concat_axis=0, tiled=True)
    phase_tile = arrived.reshape(dates * later_mates, tile_pix)
    picked = jnp.take(phase_tile, slots, axis=1)
    mapping = inverse_map(couple_entry_flags)
    velocities = jnp.dot(picked.T, mapping.T, precision=lax.Precision.HIGHEST)
    own_count = lax.dynamic_index_in_dim(block_target_totals, entry_location, 0, keepdims=False)
    valid = (jnp.arange(slot_count, dtype=jnp.int32) < own_count).astype(jnp.float32)
    return (coherence, velocities * valid[:, None])


def solution(mesh):
    in_specs = (
        P(("grp", "tile"), None, None, None),
        P("grp", None),
        P("grp"),
        P(),
        P("grp", None),
        P("grp"),
    )
    out_specs = (P(("grp", "tile"), None, None, None), P(("grp", "tile"), None))
    return jax.shard_map(local, mesh=mesh, in_specs=in_specs, out_specs=out_specs, check_vma=False)
```

profile of v0, /device:TPU:1, one launch (start us, length us, event | category | flops | bytes accessed | tf_op | source)
XLA Modules:
  0.0 134.6 jit_solution(10515715587612405986)
XLA Ops:
  0.6 2.1 %collective-permute-start = (bf16[1,2,512,512]{3,2,1,0:T(8,128)(2,1)}, bf16[1,2,512,512]{3,2,1,0:T(8,128)(2,1)}, u32[]{:S(2)}, u32[]{:S(2)}) collective-permute-start(bf16[1,2,512,512]{3,2,1,0:T(8,128)(2,1)} %param.6), channel_id=1, source_target_pairs={{1,0},{2,1},{3,2},{4,3},{5,4},{6,5},{7,6},{8,7},{9,8},{10,9},{11,1... | collective-permute-start | bytes 3145736 | tf_op jit(solution)/shard_map/ppermute | solution.py:16
  5.4 1.5 %convert_element_type.38 = f32[1,2,512,512]{3,2,1,0:T(8,128)S(1)} convert(bf16[1,2,512,512]{3,2,1,0:T(8,128)(2,1)} %param.6) | non-fusion elementwise | flops 524288 | bytes 3145728 | tf_op jit(solution)/shard_map/convert_element_type | solution.py:100
  7.5 1.4 %cholesky.16 = f32[15,15]{1,0:T(8,128)S(1)} custom-call(f32[15,15]{1,0:T(8,128)S(1)} %fusion.69), custom_call_target="Cholesky" | custom-call | tf_op jit(solution)/shard_map/jit(cholesky)/cholesky | solution.py:70
  11.7 1.3 %compare_convert_fusion = (f32[64]{0:T(128)S(1)}, pred[64]{0:T(512)(128)(4,1)S(1)}) fusion(s32[]{:T(128)} %bitcast.34, s32[16,64]{1,0:T(8,128)} %param.10, s32[]{:T(128)S(6)} %select_n.82), kind=kLoop, calls=%fused_computation.136 | loop fusion | flops 512 | bytes 584 | tf_op jit(solution)/shard_map/convert_element_type | solution.py:127
  17.6 1.3 add.193
  20.1 1.9 %reduce_sum.37 = f32[128,512]{1,0:T(8,128)S(1)} reduce(f32[128,4,512]{2,1,0:T(4,128)} %add.193, f32[]{:T(128)} %constant.122.clone.1), dimensions={1}, to_apply=%region_1.2 | reduce | flops 196608 | bytes 1310724 | tf_op jit(solution)/shard_map/reduce_sum | solution.py:29
  22.4 5.5 %collective-permute-done = bf16[1,2,512,512]{3,2,1,0:T(8,128)(2,1)} collective-permute-done((bf16[1,2,512,512]{3,2,1,0:T(8,128)(2,1)}, bf16[1,2,512,512]{3,2,1,0:T(8,128)(2,1)}, u32[]{:S(2)}, u32[]{:S(2)}) %collective-permute-start) | collective-permute-done | bytes 1048608 | tf_op jit(solution)/shard_map/ppermute | solution.py:16
  27.8 1.5 %convert_element_type.39 = f32[1,2,512,512]{3,2,1,0:T(8,128)S(1)} convert(bf16[1,2,512,512]{3,2,1,0:T(8,128)(2,1)} %collective-permute-done) | non-fusion elementwise | flops 524288 | bytes 3145728 | tf_op jit(solution)/shard_map/convert_element_type | solution.py:106
  29.4 1.3 %copy-done = f32[1,2,512,512]{3,2,1,0:T(8,128)} copy-done((f32[1,2,512,512]{3,2,1,0:T(8,128)}, f32[1,2,512,512]{3,2,1,0:T(8,128)S(1)}, u32[]{:S(2)}) %copy-start) | copy-done | bytes 2097176
  32.2 18.5 %collective-permute-done.2 = bf16[1,2,512,512]{3,2,1,0:T(8,128)(2,1)} collective-permute-done((bf16[1,2,512,512]{3,2,1,0:T(8,128)(2,1)}, bf16[1,2,512,512]{3,2,1,0:T(8,128)(2,1)}, u32[]{:S(2)}, u32[]{:S(2)}) %collective-permute-start.2) | collective-permute-done | bytes 1048608 | tf_op jit(solution)/shard_map/ppermute | solution.py:16
  50.7 1.5 %convert_element_type.41 = f32[1,2,512,512]{3,2,1,0:T(8,128)S(1)} convert(bf16[1,2,512,512]{3,2,1,0:T(8,128)(2,1)} %collective-permute-done.2) | non-fusion elementwise | flops 524288 | bytes 3145728 | tf_op jit(solution)/shard_map/convert_element_type | solution.py:106
  53.4 1.5 %convert_element_type.40 = f32[1,2,512,512]{3,2,1,0:T(8,128)S(1)} convert(bf16[1,2,512,512]{3,2,1,0:T(8,128)(2,1)} %collective-permute-done.1) | non-fusion elementwise | flops 524288 | bytes 3145728 | tf_op jit(solution)/shard_map/convert_element_type | solution.py:106
  55.2 1.3 copy-done.1
  56.8 13.0 %fusion.4 = (f32[512,512]{1,0:T(8,128)}, f32[1,1,512,512]{3,2,1,0:T(8,128)S(1)}, f32[1,1,512,512]{3,2,1,0:T(8,128)S(1)}, f32[512,512]{1,0:T(8,128)}, f32[1,1,512...) fusion(f32[512,512]{1,0:T(8,128)S(1)} %copy-done.10, ...), kind=kLoop, calls=%fused_computation.19 | loop fusion | flops 7864320 | bytes 18874380 | tf_op jit(solution)/shard_map/add | solution.py:44
  69.8 12.5 %fusion.5 = (f32[512,512]{1,0:T(8,128)}, f32[512,512]{1,0:T(8,128)}, f32[512,512]{1,0:T(8,128)}) fusion(f32[1,1,512,512]{3,2,1,0:T(8,128)S(1)} %get-tuple-element.4, f32[1,1,512,512]{3,2,1,0:T(8,128)S(1)} %get-tuple-element.3, f32[512,512]{1,0:T(8,128)S(1)} %copy-done.10, f32[]{:T(128)} %bitcast.1, f32[1,1,512,512]{3,2,1,0:T(8,128)S(1)} %get-tuple-element.16, ...), kind=kLoop, calls=%fused_computation.20 | loop fusion | flops 3145728 | bytes 10485772 | tf_op jit(solution)/shard_map/sub | solution.py:45
  82.3 2.7 %stack.61 = f32[1,128,4,512]{3,2,1,0:T(4,128)} reshape(f32[512,512]{1,0:T(8,128)} %get-tuple-element.17) | data formatting | bytes 2097152 | tf_op jit(solution)/shard_map/stack | solution.py:47
  87.6 2.7 %stack.71 = f32[1,128,4,512]{3,2,1,0:T(4,128)} reshape(f32[512,512]{1,0:T(8,128)} %get-tuple-element.19) | data formatting | bytes 2097152 | tf_op jit(solution)/shard_map/stack | solution.py:47
  91.6 3.9 %maximum_reduce_fusion = f32[3,128,512]{2,1,0:T(8,128)S(1)} fusion(f32[1,128,4,512]{3,2,1,0:T(4,128)S(1)} %copy-done.6, f32[1,128,4,512]{3,2,1,0:T(4,128)} %stack.61, f32[1,128,4,512]{3,2,1,0:T(4,128)} %stack.60), kind=kLoop, calls=%fused_computation.1 | loop fusion | flops 2162688 | bytes 3932160 | tf_op jit(solution)/shard_map/reduce_sum | solution.py:29
  96.4 2.2 %maximum_reduce_fusion.2 = f32[3,128,512]{2,1,0:T(8,128)S(1)} fusion(f32[1,128,4,512]{3,2,1,0:T(4,128)S(1)} %copy-done.7, f32[1,128,4,512]{3,2,1,0:T(4,128)S(1)} %copy-done.8, f32[1,128,4,512]{3,2,1,0:T(4,128)S(1)} %copy-done.9), kind=kLoop, calls=%fused_computation.3 | loop fusion | flops 2162688 | bytes 3932160 | tf_op jit(solution)/shard_map/reduce_sum | solution.py:29
  99.7 1.5 %stack.66 = f32[1,128,4,512]{3,2,1,0:T(4,128)S(1)} reshape(f32[512,512]{1,0:T(8,128)} %get-tuple-element.18) | data formatting | bytes 2097152 | tf_op jit(solution)/shard_map/stack | solution.py:47
  101.3 1.3 stack.65
  102.6 3.4 %maximum_reduce_fusion.1 = f32[3,128,512]{2,1,0:T(8,128)S(1)} fusion(f32[1,128,4,512]{3,2,1,0:T(4,128)S(1)} %stack.67, f32[1,128,4,512]{3,2,1,0:T(4,128)S(1)} %stack.66, f32[1,128,4,512]{3,2,1,0:T(4,128)} %stack.65), kind=kLoop, calls=%fused_computation.2 | loop fusion | flops 2162688 | bytes 3932160 | tf_op jit(solution)/shard_map/reduce_sum | solution.py:29
  109.9 16.0 %all-to-all-start = ((f32[16,1,768]{2,1,0:T(1,128)}), f32[16,1,768]{2,1,0:T(1,128)S(1)}, u32[]{:S(2)}, u32[]{:S(2)}) async-start(f32[16,1,768]{2,1,0:T(1,128)} %reshape.283), calls=%async_computation | async-start | bytes 98304 | tf_op jit(solution)/shard_map/all_to_all | solution.py:121
  126.5 5.3 %all-to-all-done = f32[16,1,768]{2,1,0:T(1,128)S(1)} async-done(((f32[16,1,768]{2,1,0:T(1,128)}), f32[16,1,768]{2,1,0:T(1,128)S(1)}, u32[]{:S(2)}, u32[]{:S(2)}) %all-to-all-start) | async-done | bytes 49184 | tf_op jit(solution)/shard_map/all_to_all | solution.py:121
  (75 shorter events, 24.8 us)
Async XLA Ops:
  0.6 6.3 %copy-start.11 = (s32[16,3]{0,1:T(4,128)S(1)}, s32[16,3]{0,1:T(4,128)}, u32[]{:S(2)}) copy-start(s32[16,3]{0,1:T(4,128)} %param.9) | copy-start | bytes 580
  0.6 9.6 %copy-start.13 = (s32[16]{0:T(128)S(1)}, s32[16]{0:T(128)}, u32[]{:S(2)}) copy-start(s32[16]{0:T(128)} %param.11) | copy-start | bytes 196
  0.6 27.2 %collective-permute-start = (bf16[1,2,512,512]{3,2,1,0:T(8,128)(2,1)}, bf16[1,2,512,512]{3,2,1,0:T(8,128)(2,1)}, u32[]{:S(2)}, u32[]{:S(2)}) collective-permute-start(bf16[1,2,512,512]{3,2,1,0:T(8,128)(2,1)} %param.6), channel_id=1, source_target_pairs={{1,0},{2,1},{3,2},{4,3},{5,4},{6,5},{7,6},{8,7},{9,8},{10,9},{11,1... | collective-permute-start | bytes 3145736 | tf_op jit(solution)/shard_map/ppermute | solution.py:16
  2.8 48.0 %collective-permute-start.2 = (bf16[1,2,512,512]{3,2,1,0:T(8,128)(2,1)}, bf16[1,2,512,512]{3,2,1,0:T(8,128)(2,1)}, u32[]{:S(2)}, u32[]{:S(2)}) collective-permute-start(bf16[1,2,512,512]{3,2,1,0:T(8,128)(2,1)} %param.6), channel_id=1, source_target_pairs={{3,0},{4,1},{5,2},{6,3},{7,4},{8,5},{9,6},{10,7},{11,8},{12,9},{13... | collective-permute-start | bytes 3145736 | tf_op jit(solution)/shard_map/ppermute | solution.py:16
  4.1 49.4 %collective-permute-start.1 = (bf16[1,2,512,512]{3,2,1,0:T(8,128)(2,1)}, bf16[1,2,512,512]{3,2,1,0:T(8,128)(2,1)}, u32[]{:S(2)}, u32[]{:S(2)}) collective-permute-start(bf16[1,2,512,512]{3,2,1,0:T(8,128)(2,1)} %param.6), channel_id=1, source_target_pairs={{2,0},{3,1},{4,2},{5,3},{6,4},{7,5},{8,6},{9,7},{10,8},{11,9},{12,... | collective-permute-start | bytes 3145736 | tf_op jit(solution)/shard_map/ppermute | solution.py:16
  6.9 6.4 %copy-start.12 = (f32[16]{0:T(128)S(1)}, f32[16]{0:T(128)}, u32[]{:S(2)}) copy-start(f32[16]{0:T(128)} %param.8) | copy-start | bytes 196
  29.4 1.4 %copy-start = (f32[1,2,512,512]{3,2,1,0:T(8,128)}, f32[1,2,512,512]{3,2,1,0:T(8,128)S(1)}, u32[]{:S(2)}) copy-start(f32[1,2,512,512]{3,2,1,0:T(8,128)S(1)} %convert_element_type.39) | copy-start | bytes 6291460
  55.0 1.6 %copy-start.1 = (f32[1,2,512,512]{3,2,1,0:T(8,128)S(1)}, f32[1,2,512,512]{3,2,1,0:T(8,128)}, u32[]{:S(2)}) copy-start(f32[1,2,512,512]{3,2,1,0:T(8,128)} %copy-done) | copy-start | bytes 6291460
  55.0 1.9 %copy-start.10 = (f32[512,512]{1,0:T(8,128)S(1)}, f32[512,512]{1,0:T(8,128)}, u32[]{:S(2)}) copy-start(f32[512,512]{1,0:T(8,128)} %param.7) | copy-start | bytes 3145732
  82.3 2.7 %copy-start.5 = (f32[512,512]{1,0:T(8,128)S(1)}, f32[512,512]{1,0:T(8,128)}, u32[]{:S(2)}) copy-start(f32[512,512]{1,0:T(8,128)} %get-tuple-element.2) | copy-start | bytes 3145732
  82.3 4.0 %copy-start.3 = (f32[1,1,512,512]{3,2,1,0:T(8,128)S(1)}, f32[1,1,512,512]{3,2,1,0:T(8,128)}, u32[]{:S(2)}) copy-start(f32[1,1,512,512]{3,2,1,0:T(8,128)} %multiply_add_fusion) | copy-start | bytes 3145732
  86.3 4.0 %copy-start.4 = (f32[512,512]{1,0:T(8,128)S(1)}, f32[512,512]{1,0:T(8,128)}, u32[]{:S(2)}) copy-start(f32[512,512]{1,0:T(8,128)} %get-tuple-element.11) | copy-start | bytes 3145732
  87.6 4.0 %copy-start.6 = (f32[1,128,4,512]{3,2,1,0:T(4,128)S(1)}, f32[1,128,4,512]{3,2,1,0:T(4,128)}, u32[]{:S(2)}) copy-start(f32[1,128,4,512]{3,2,1,0:T(4,128)} %stack.62) | copy-start | bytes 3145732
  91.6 4.8 %copy-start.7 = (f32[1,128,4,512]{3,2,1,0:T(4,128)S(1)}, f32[1,128,4,512]{3,2,1,0:T(4,128)}, u32[]{:S(2)}) copy-start(f32[1,128,4,512]{3,2,1,0:T(4,128)} %stack.72) | copy-start | bytes 3145732
  91.6 4.8 %copy-start.8 = (f32[1,128,4,512]{3,2,1,0:T(4,128)S(1)}, f32[1,128,4,512]{3,2,1,0:T(4,128)}, u32[]{:S(2)}) copy-start(f32[1,128,4,512]{3,2,1,0:T(4,128)} %stack.71) | copy-start | bytes 3145732
  91.6 4.8 %copy-start.9 = (f32[1,128,4,512]{3,2,1,0:T(4,128)S(1)}, f32[1,128,4,512]{3,2,1,0:T(4,128)}, u32[]{:S(2)}) copy-start(f32[1,128,4,512]{3,2,1,0:T(4,128)} %stack.70) | copy-start | bytes 3145732
  99.4 1.9 %copy-start.2 = (f32[512,512]{1,0:T(8,128)S(1)}, f32[512,512]{1,0:T(8,128)}, u32[]{:S(2)}) copy-start(f32[512,512]{1,0:T(8,128)} %get-tuple-element.14) | copy-start | bytes 3145732
  109.9 21.9 %all-to-all-start = ((f32[16,1,768]{2,1,0:T(1,128)}), f32[16,1,768]{2,1,0:T(1,128)S(1)}, u32[]{:S(2)}, u32[]{:S(2)}) async-start(f32[16,1,768]{2,1,0:T(1,128)} %reshape.283), calls=%async_computation | async-start | bytes 98304 | tf_op jit(solution)/shard_map/all_to_all | solution.py:121
where the time goes:
time: 136 us; the launch traced here: 135 us
  other arithmetic  53.6 us (39%)
  waiting for transfers between devices  29.2 us (21%)
  local copies, waits for them, and re-layouts  22.2 us (16%)
  starting transfers between devices  20.6 us (15%)
  between operations  4.67 us (3%)
  matrix products  4.33 us (3%)
    ppermute x3, waiting for transfers between devices, from_behind(): return lax.ppermute(block, axis, route)  24 us
    all_to_all x1, starting transfers between devices, local(): lax.all_to_all(phase_local, 'tile', split_axis=2, concat_axis=0, tiled=True)  16 us
    another operation x9, local copies, waits for them, and re-layouts, pair_stats(): jnp.stack([flat_real, flat_imag, other_energy], axis=0)  13.6 us
    add x1, other arithmetic, pair_stats(): flat_real = cross_real * cosine + cross_imag * sine  13 us
    sub x1, other arithmetic, pair_stats(): flat_imag = cross_imag * cosine - cross_real * sine  12.5 us
    reduce_sum x4, other arithmetic, looked(): jnp.sum(field.reshape(field.shape[:-2] + (rows // LOOK_ROWS, LOOK_ROWS, c...  11.4 us
    all_to_all x1, waiting for transfers between devices, local(): lax.all_to_all(phase_local, 'tile', split_axis=2, concat_axis=0, tiled=True)  5.29 us
    ppermute x3, starting transfers between devices, from_behind(): return lax.ppermute(block, axis, route)  4.68 us
  transfers between devices with their start and end apart: 4, of which 3 were waited for; matrix products, arithmetic and copies ran while one was open for 15% of the time, Pallas kernels for 0%

commit v1 on v0

v1 whole, which is shorter than its diff:
```python
import functools

import jax
import jax.numpy as jnp
from jax import lax
from jax.experimental import pallas as pl
from jax.experimental.pallas import tpu as pltpu
from jax.sharding import PartitionSpec as P

LOOK_ROWS = 4
LOOK_COLS = 16
LANES = 128
EPSILON = 1e-06
HIGHEST = lax.Precision.HIGHEST


def iota(shape, axis):
    return lax.broadcasted_iota(jnp.int32, shape, axis)


def sine_cosine(x):
    turns = jnp.round(x * 0.6366197723675814)
    r = (x - turns * 1.5703125) - turns * 4.838267948966e-4
    z = r * r
    s = r + r * z * (-1.6666654611e-1 + z * (8.3321608736e-3 + z * -1.9515295891e-4))
    c = 1.0 - 0.5 * z + z * z * (
        4.166664568298827e-2 + z * (-1.388731625493765e-3 + z * 2.443315711809948e-5)
    )
    quarter = turns.astype(jnp.int32)
    odd = (quarter & 1) == 1
    sine = jnp.where(odd, c, s) * (1 - (quarter & 2)).astype(jnp.float32)
    cosine = jnp.where(odd, s, c) * (1 - ((quarter + 1) & 2)).astype(jnp.float32)
    return sine, cosine


def inverse_map(flags, dates, mates):
    intervals = dates - 1
    rows = -(-intervals // 8) * 8
    pairs = -(-dates * mates // LANES) * LANES
    slot = iota((dates, pairs), 1)
    spread = jnp.zeros((dates, pairs), jnp.float32)
    for k in range(mates):
        spread = spread + jnp.where(slot % mates == k, flags[:, k : k + 1].astype(jnp.float32), 0.0)
    used = jnp.sum(
        jnp.where(slot // mates == iota((dates, pairs), 0), spread, 0.0), axis=0, keepdims=True
    )
    interval = iota((rows, pairs), 0)
    pair = iota((rows, pairs), 1)
    first = pair // mates
    covered = (interval >= first) & (interval < first + pair % mates + 1) & (interval < intervals)
    right = jnp.where(covered, used, 0.0)
    normal = lax.dot_general(
        right.astype(jnp.bfloat16),
        right.astype(jnp.bfloat16),
        (((1,), (1,)), ((), ())),
        preferred_element_type=jnp.float32,
    )
    down = iota((rows, rows), 0)
    across = iota((rows, rows), 1)
    down_right = iota((rows, pairs), 0)

    def eliminate(t, carry):
        a, b = carry
        row_a = jnp.sum(jnp.where(down == t, a, 0.0), axis=0, keepdims=True)
        row_b = jnp.sum(jnp.where(down_right == t, b, 0.0), axis=0, keepdims=True)
        column = jnp.sum(jnp.where(across == t, a, 0.0), axis=1, keepdims=True)
        pivot = jnp.sum(jnp.where(across[:1] == t, row_a, 0.0), axis=1, keepdims=True)
        row_a = row_a / pivot
        row_b = row_b / pivot
        return (
            jnp.where(down == t, row_a, a - column * row_a),
            jnp.where(down_right == t, row_b, b - column * row_b),
        )

    return lax.fori_loop(0, intervals, eliminate, (normal, right))[1]


def kernel(
    dates,
    mates,
    frames,
    heights,
    spacings,
    flags_scalar,
    flags_vector,
    targets,
    totals,
    coherence,
    velocities,
    held,
    height_rows,
    natural,
    height_looks,
    rotated,
    powers,
    phases,
    coh,
    send_sem,
    recv_sem,
    coh_send_sem,
    coh_recv_sem,
    local_sem,
):
    me = lax.axis_index("tile")
    rows = held.shape[2]
    cols = held.shape[3]
    tiles = cols // LANES
    looks = rows // LOOK_ROWS
    looked_cols = cols // LOOK_COLS
    pairs = dates * mates
    slots = targets.shape[1]
    window = rotated.shape[0]

    own_rows = pl.ds(pl.multiple_of(me * rows, rows), rows)
    own_block = pltpu.make_async_copy(frames.at[0, :, own_rows, :], held.at[me], local_sem.at[0])
    own_heights = pltpu.make_async_copy(heights.at[own_rows, :], height_rows, local_sem.at[1])
    own_block.start()
    own_heights.start()

    barrier = pltpu.get_barrier_semaphore()

    def greet(step, carry):
        pl.semaphore_signal(
            barrier,
            inc=1,
            device_id={"tile": (me + step) % dates},
            device_id_type=pl.DeviceIdType.MESH,
        )
        return carry

    lax.fori_loop(1, dates, greet, 0)
    pl.semaphore_wait(barrier, dates - 1)

    def image_copy(to, date):
        return pltpu.make_async_remote_copy(
            src_ref=frames.at[0, :, pl.ds(pl.multiple_of(to * rows, rows), rows), :],
            dst_ref=held.at[date],
            send_sem=send_sem.at[to],
            recv_sem=recv_sem.at[date],
            device_id={"tile": to},
            device_id_type=pl.DeviceIdType.MESH,
        )

    def send_image(step, carry):
        image_copy((me + step) % dates, me).start()
        return carry

    lax.fori_loop(1, dates, send_image, 0)

    def coh_copy(to, tile):
        return pltpu.make_async_remote_copy(
            src_ref=coh.at[to],
            dst_ref=coherence.at[0, :, pl.ds(pl.multiple_of(tile * looks, looks), looks), :],
            send_sem=coh_send_sem.at[to],
            recv_sem=coh_recv_sem.at[tile],
            device_id={"tile": to},
            device_id_type=pl.DeviceIdType.MESH,
        )

    own_coh = pltpu.make_async_copy(
        coh.at[me],
        coherence.at[0, :, pl.ds(pl.multiple_of(me * looks, looks), looks), :],
        local_sem.at[2],
    )

    def hand_out(date):
        @pl.when(date == me)
        def _():
            own_coh.start()

        @pl.when(date != me)
        def _():
            coh_copy(date, me).start()

    rotated[...] = jnp.zeros_like(rotated)
    powers[...] = jnp.zeros_like(powers)
    phases[...] = jnp.zeros_like(phases)
    coh[...] = jnp.zeros_like(coh)

    mapping = inverse_map(flags_vector[...], dates, mates)

    look_lane = iota((cols, LANES), 1)
    pooling = jnp.where(
        iota((cols, LANES), 0) // LOOK_COLS == look_lane, 1.0 / (LOOK_ROWS * LOOK_COLS), 0.0
    ).astype(jnp.bfloat16)

    own_block.wait()
    own_heights.wait()
    for c in range(tiles):
        natural[0, c] = height_rows[:, c * LANES : (c + 1) * LANES]
    for j in range(LOOK_ROWS):
        height_looks[j] = natural[0, :, pl.ds(j, looks, stride=LOOK_ROWS), :]

    def one_date(date, carry):
        @pl.when(date != me)
        def _():
            image_copy(date, date).wait_recv()

        place = date % window
        for plane in range(2):
            for c in range(tiles):
                natural[plane, c] = held[date, plane, :, c * LANES : (c + 1) * LANES].astype(
                    jnp.float32
                )
        spacing = spacings[date]
        power = None
        for j in range(LOOK_ROWS):
            real = natural[0, :, pl.ds(j, looks, stride=LOOK_ROWS), :]
            imag = natural[1, :, pl.ds(j, looks, stride=LOOK_ROWS), :]
            sine, cosine = sine_cosine(spacing * height_looks[j])
            rotated[place, 0, j] = real * cosine + imag * sine
            rotated[place, 1, j] = imag * cosine - real * sine
            energy = real * real + imag * imag
            power = energy if j == 0 else power + energy
        fields = [power]
        for k in range(1, mates + 1):
            other = (date + window - k) % window
            flat_real = 0.0
            flat_imag = 0.0
            for j in range(LOOK_ROWS):
                a_real = rotated[other, 0, j]
                a_imag = rotated[other, 1, j]
                c_real = rotated[place, 0, j]
                c_imag = rotated[place, 1, j]
                flat_real = flat_real + (a_real * c_real + a_imag * c_imag)
                flat_imag = flat_imag + (a_imag * c_real - a_real * c_imag)
            fields += [flat_real, flat_imag]
        sums = jnp.concatenate(
            [jnp.concatenate([field[c] for c in range(tiles)], axis=1) for field in fields], axis=0
        )
        high = sums.astype(jnp.bfloat16).astype(jnp.float32)
        split = jnp.concatenate([high, sums - high], axis=0).astype(jnp.bfloat16)
        pooled = jnp.dot(split, pooling, preferred_element_type=jnp.float32)
        means = pooled[: sums.shape[0]] + pooled[sums.shape[0] :]
        power_other = means[:looks]
        powers[place] = power_other
        for k in range(1, mates + 1):
            mean_real = means[(2 * k - 1) * looks : 2 * k * looks]
            mean_imag = means[2 * k * looks : (2 * k + 1) * looks]
            power_own = powers[(date + window - k) % window]
            scale = 1.0 / jnp.sqrt(power_own * power_other + EPSILON)
            amplitude = jnp.sqrt(mean_real * mean_real + mean_imag * mean_imag) * scale

            @pl.when(date >= k)
            def _():
                flag = flags_scalar[date - k, k - 1].astype(jnp.float32)
                coh[date - k, k - 1] = (amplitude * flag)[:, :looked_cols]
                phases[(date - k) * mates + (k - 1)] = mean_imag * scale

        @pl.when(date >= mates)
        def _():
            hand_out(date - mates)

        return carry

    lax.fori_loop(0, dates, one_date, 0)
    lax.fori_loop(dates - mates, dates, lambda date, carry: (hand_out(date), carry)[1], 0)

    listed = targets[pl.ds(me, 1), :]
    diagonal = iota((slots, slots), 0) == iota((slots, slots), 1)
    row_of = (listed // looked_cols).astype(jnp.float32)
    column_of = (listed % looked_cols).astype(jnp.float32)
    row_down = jnp.sum(jnp.where(diagonal, row_of, 0.0), axis=1, keepdims=True)
    column_down = jnp.sum(jnp.where(diagonal, column_of, 0.0), axis=1, keepdims=True)
    by_column = jnp.where(
        iota((slots, LANES), 1).astype(jnp.float32) == column_down, 1.0, 0.0
    )
    flat_phases = phases[...].reshape(pairs * looks, LANES)
    rows_picked = lax.dot_general(
        by_column,
        flat_phases,
        (((1,), (1,)), ((), ())),
        precision=HIGHEST,
        preferred_element_type=jnp.float32,
    )
    lane = iota((slots, pairs * looks), 1)
    picked = jnp.where((lane % looks).astype(jnp.float32) == row_down, rows_picked, 0.0)
    expand = jnp.where(
        iota((mapping.shape[1], pairs * looks), 1) // looks
        == iota((mapping.shape[1], pairs * looks), 0),
        1.0,
        0.0,
    )
    wide = jnp.dot(mapping, expand, precision=HIGHEST, preferred_element_type=jnp.float32)
    result = lax.dot_general(
        picked,
        wide,
        (((1,), (1,)), ((), ())),
        precision=HIGHEST,
        preferred_element_type=jnp.float32,
    )
    result = jnp.where(iota(result.shape, 0) < totals[me], result, 0.0)
    velocities[...] = result[:, : dates - 1]

    own_coh.wait()

    def finish(step, carry):
        other = (me + step) % dates
        image_copy(other, me).wait_send()
        coh_copy(other, me).wait_send()
        coh_copy(other, other).wait_recv()
        return carry

    lax.fori_loop(1, dates, finish, 0)


def local(
    full_resolution_frames,
    height_angle_factor,
    normal_spacings,
    couple_entry_flags,
    block_target_indices,
    block_target_totals,
):
    dates, mates = couple_entry_flags.shape
    image_rows, cols = height_angle_factor.shape
    rows = image_rows // dates
    tiles = cols // LANES
    looks = rows // LOOK_ROWS
    looked_cols = cols // LOOK_COLS
    slots = block_target_indices.shape[1]
    window = mates + 1
    f32 = jnp.float32
    vmem = pl.BlockSpec(memory_space=pltpu.VMEM)
    smem = pl.BlockSpec(memory_space=pltpu.SMEM)
    anywhere = pl.BlockSpec(memory_space=pl.ANY)
    return pl.pallas_call(
        functools.partial(kernel, dates, mates),
        out_shape=(
            jax.ShapeDtypeStruct((1, mates, image_rows // LOOK_ROWS, looked_cols), f32),
            jax.ShapeDtypeStruct((slots, dates - 1), f32),
        ),
        in_specs=[anywhere, anywhere, smem, smem, vmem, vmem, smem],
        out_specs=(vmem, vmem),
        scratch_shapes=[
            pltpu.VMEM((dates, 2, rows, cols), jnp.bfloat16),
            pltpu.VMEM((rows, cols), f32),
            pltpu.VMEM((2, tiles, rows, LANES), f32),
            pltpu.VMEM((LOOK_ROWS, tiles, looks, LANES), f32),
            pltpu.VMEM((window, 2, LOOK_ROWS, tiles, looks, LANES), f32),
            pltpu.VMEM((window, looks, LANES), f32),
            pltpu.VMEM((dates * mates, looks, LANES), f32),
            pltpu.VMEM((dates, mates, looks, looked_cols), f32),
            pltpu.SemaphoreType.DMA((dates,)),
            pltpu.SemaphoreType.DMA((dates,)),
            pltpu.SemaphoreType.DMA((dates,)),
            pltpu.SemaphoreType.DMA((dates,)),
            pltpu.SemaphoreType.DMA((3,)),
        ],
        compiler_params=pltpu.CompilerParams(
            collective_id=0, has_side_effects=True, vmem_limit_bytes=40 * 1024 * 1024
        ),
    )(
        full_resolution_frames,
        height_angle_factor,
        normal_spacings,
        couple_entry_flags,
        couple_entry_flags,
        block_target_indices,
        block_target_totals,
    )


def solution(mesh):
    in_specs = (
        P(("grp", "tile"), None, None, None),
        P("grp", None),
        P("grp"),
        P(),
        P("grp", None),
        P("grp"),
    )
    out_specs = (P(("grp", "tile"), None, None, None), P(("grp", "tile"), None))
    return jax.shard_map(local, mesh=mesh, in_specs=in_specs, out_specs=out_specs, check_vma=False)
```

time: 136 us -> 44.3 us (0.33)
  the two profiles are of different devices: /device:TPU:1 before, /device:TPU:27 now
where the time goes in v1:
time: 44.3 us; the launch traced here: 44 us
  Pallas kernels  38.7 us (87%)
  local copies, waits for them, and re-layouts  4.64 us (10%)
  between operations  0.68 us (2%)
    pallas_call x1, Pallas kernels, local(): pl.pallas_call(functools.partial(kernel, dates, mates), out_shape=(jax.Sh...  38.7 us
    unnamed x11, local copies, waits for them, and re-layouts  3.23 us
    pallas_call x2, local copies, waits for them, and re-layouts, local(): pl.pallas_call(functools.partial(kernel, dates, mates), out_shape=(jax.Sh...  1.4 us

profile of v1, /device:TPU:27, one launch (start us, length us, event | category | flops | bytes accessed | tf_op | source)
XLA Modules:
  0.0 44.0 jit_solution(5896499810933903900)
XLA Ops:
  0.6 0.0 copy-start.4
  0.6 0.0 copy-start.2
  0.7 0.0 copy-start.3
  0.7 0.8 %copy.8.flags_scalar.flags_vector = s32[16,3]{1,0:T(8,128)S(1)} copy(s32[16,3]{0,1:T(4,128)} %param.9) | data formatting | bytes 384 | tf_op args[3]
  1.4 0.0 copy-done.4
  1.4 0.0 copy-done.2
  1.4 0.0 copy-done.3
  1.4 0.0 copy-start
  1.5 1.2 %copy-done = bf16[1,2,512,512]{3,2,1,0:T(8,128)(2,1)S(1)} copy-done((bf16[1,2,512,512]{3,2,1,0:T(8,128)(2,1)S(1)}, bf16[1,2,512,512]{3,2,1,0:T(8,128)(2,1)}, u32[]{:S(2)}) %copy-start) | copy-done | bytes 1048600
  2.7 0.0 copy-start.1
  2.7 1.2 %copy-done.1 = f32[512,512]{1,0:T(8,128)S(1)} copy-done((f32[512,512]{1,0:T(8,128)S(1)}, f32[512,512]{1,0:T(8,128)}, u32[]{:S(2)}) %copy-start.1) | copy-done | bytes 1048600
  3.9 38.7 %shard_map.77 = (f32[1,3,128,32]{3,2,1,0:T(8,128)S(1)}, f32[64,15]{1,0:T(8,128)S(1)}) custom-call(bf16[1,2,512,512]{3,2,1,0:T(8,128)(2,1)S(1)} %copy-done, f32[512,512]{1,0:T(8,128)S(1)} %copy-done.1, f32[16]{0:T(128)S(1)} %copy-done.3, s32[16,3]{1,0:T(8,128)S(1)} %copy.8.flags_scalar.flags_vector, s32[16,3]{1,0:T(8,128)S(1)} %copy.8.flags_scalar.flags_vector, ...), custom_call_target="tpu_custom_call" | custom-call | tf_op jit(solution)/shard_map/pallas_call | solution.py:327
  42.6 0.7 %copy.10 = f32[1,3,128,32]{2,3,1,0:T(8,128)} copy(f32[1,3,128,32]{3,2,1,0:T(8,128)S(1)} %get-tuple-element.2) | data formatting | bytes 98304 | tf_op jit(solution)/shard_map/pallas_call | solution.py:327
  43.4 0.7 %copy.11 = f32[64,15]{0,1:T(8,128)} copy(f32[64,15]{1,0:T(8,128)S(1)} %get-tuple-element.3) | data formatting | bytes 7680 | tf_op jit(solution)/shard_map/pallas_call | solution.py:327
Async XLA Ops:
  0.6 0.8 %copy-start.4 = (s32[16]{0:T(128)S(1)}, s32[16]{0:T(128)}, u32[]{:S(2)}) copy-start(s32[16]{0:T(128)} %totals.1) | copy-start | bytes 196
  0.6 0.8 %copy-start.2 = (s32[16,64]{1,0:T(8,128)S(1)}, s32[16,64]{1,0:T(8,128)}, u32[]{:S(2)}) copy-start(s32[16,64]{1,0:T(8,128)} %targets.1) | copy-start | bytes 12292
  0.7 0.8 %copy-start.3 = (f32[16]{0:T(128)S(1)}, f32[16]{0:T(128)}, u32[]{:S(2)}) copy-start(f32[16]{0:T(128)} %spacings.1) | copy-start | bytes 196
  1.4 1.2 %copy-start = (bf16[1,2,512,512]{3,2,1,0:T(8,128)(2,1)S(1)}, bf16[1,2,512,512]{3,2,1,0:T(8,128)(2,1)}, u32[]{:S(2)}) copy-start(bf16[1,2,512,512]{3,2,1,0:T(8,128)(2,1)} %frames.1) | copy-start | bytes 3145732
  2.7 1.2 %copy-start.1 = (f32[512,512]{1,0:T(8,128)S(1)}, f32[512,512]{1,0:T(8,128)}, u32[]{:S(2)}) copy-start(f32[512,512]{1,0:T(8,128)} %heights.1) | copy-start | bytes 3145732

commit v2 on v1

--- a/solution.py
+++ b/solution.py
@@ -37,13 +37,14 @@
     intervals = dates - 1
     rows = -(-intervals // 8) * 8
     pairs = -(-dates * mates // LANES) * LANES
-    slot = iota((dates, pairs), 1)
-    spread = jnp.zeros((dates, pairs), jnp.float32)
-    for k in range(mates):
-        spread = spread + jnp.where(slot % mates == k, flags[:, k : k + 1].astype(jnp.float32), 0.0)
-    used = jnp.sum(
-        jnp.where(slot // mates == iota((dates, pairs), 0), spread, 0.0), axis=0, keepdims=True
-    )
+    own_slot = iota((dates, pairs), 1) // mates == iota((dates, pairs), 0)
+    spread = jnp.dot(
+        flags.astype(jnp.bfloat16),
+        jnp.where(own_slot, 1.0, 0.0).astype(jnp.bfloat16),
+        preferred_element_type=jnp.float32,
+    )
+    kind = iota((mates, pairs), 1) % mates == iota((mates, pairs), 0)
+    used = jnp.sum(jnp.where(kind, spread, 0.0), axis=0, keepdims=True)
     interval = iota((rows, pairs), 0)
     pair = iota((rows, pairs), 1)
     first = pair // mates
@@ -95,6 +96,7 @@
     powers,
     phases,
     coh,
+    gathered,
     send_sem,
     recv_sem,
     coh_send_sem,
@@ -131,6 +133,9 @@
     lax.fori_loop(1, dates, greet, 0)
     pl.semaphore_wait(barrier, dates - 1)
 
+    def partner(step):
+        return me ^ step if dates & (dates - 1) == 0 else (me + step) % dates
+
     def image_copy(to, date):
         return pltpu.make_async_remote_copy(
             src_ref=frames.at[0, :, pl.ds(pl.multiple_of(to * rows, rows), rows), :],
@@ -142,7 +147,7 @@
         )
 
     def send_image(step, carry):
-        image_copy((me + step) % dates, me).start()
+        image_copy(partner(dates - step), me).start()
         return carry
 
     lax.fori_loop(1, dates, send_image, 0)
@@ -150,7 +155,7 @@
     def coh_copy(to, tile):
         return pltpu.make_async_remote_copy(
             src_ref=coh.at[to],
-            dst_ref=coherence.at[0, :, pl.ds(pl.multiple_of(tile * looks, looks), looks), :],
+            dst_ref=gathered.at[pl.ds(pl.multiple_of(tile * looks, looks), looks), :],
             send_sem=coh_send_sem.at[to],
             recv_sem=coh_recv_sem.at[tile],
             device_id={"tile": to},
@@ -159,7 +164,7 @@
 
     own_coh = pltpu.make_async_copy(
         coh.at[me],
-        coherence.at[0, :, pl.ds(pl.multiple_of(me * looks, looks), looks), :],
+        gathered.at[pl.ds(pl.multiple_of(me * looks, looks), looks), :],
         local_sem.at[2],
     )
 
@@ -176,6 +181,7 @@
     powers[...] = jnp.zeros_like(powers)
     phases[...] = jnp.zeros_like(phases)
     coh[...] = jnp.zeros_like(coh)
+    assert mates * looked_cols <= LANES
 
     mapping = inverse_map(flags_vector[...], dates, mates)
 
@@ -243,8 +249,11 @@
 
             @pl.when(date >= k)
             def _():
-                flag = flags_scalar[date - k, k - 1].astype(jnp.float32)
-                coh[date - k, k - 1] = (amplitude * flag)[:, :looked_cols]
+                flag = flags_scalar[k - 1, date - k].astype(jnp.float32)
+                shown = amplitude * flag
+                if k > 1:
+                    shown = coh[date - k] + pltpu.roll(shown, (k - 1) * looked_cols, 1)
+                coh[date - k] = shown
                 phases[(date - k) * mates + (k - 1)] = mean_imag * scale
 
         @pl.when(date >= mates)
@@ -283,14 +292,14 @@
     )
     wide = jnp.dot(mapping, expand, precision=HIGHEST, preferred_element_type=jnp.float32)
     result = lax.dot_general(
+        wide,
         picked,
-        wide,
         (((1,), (1,)), ((), ())),
         precision=HIGHEST,
         preferred_element_type=jnp.float32,
     )
-    result = jnp.where(iota(result.shape, 0) < totals[me], result, 0.0)
-    velocities[...] = result[:, : dates - 1]
+    result = jnp.where(iota(result.shape, 1) < totals[me], result, 0.0)
+    velocities[...] = result[: dates - 1]
 
     own_coh.wait()
 
@@ -302,6 +311,9 @@
         return carry
 
     lax.fori_loop(1, dates, finish, 0)
+    across_rows = jnp.transpose(gathered[...])
+    for k in range(mates):
+        coherence[0, k] = across_rows[k * looked_cols : (k + 1) * looked_cols]
 
 
 def local(
@@ -323,14 +335,14 @@
     f32 = jnp.float32
     vmem = pl.BlockSpec(memory_space=pltpu.VMEM)
     smem = pl.BlockSpec(memory_space=pltpu.SMEM)
-    anywhere = pl.BlockSpec(memory_space=pl.ANY)
-    return pl.pallas_call(
+    hbm = pl.BlockSpec(memory_space=pltpu.HBM)
+    coherence, velocities = pl.pallas_call(
         functools.partial(kernel, dates, mates),
         out_shape=(
-            jax.ShapeDtypeStruct((1, mates, image_rows // LOOK_ROWS, looked_cols), f32),
-            jax.ShapeDtypeStruct((slots, dates - 1), f32),
+            jax.ShapeDtypeStruct((1, mates, looked_cols, image_rows // LOOK_ROWS), f32),
+            jax.ShapeDtypeStruct((dates - 1, slots), f32),
         ),
-        in_specs=[anywhere, anywhere, smem, smem, vmem, vmem, smem],
+        in_specs=[hbm, hbm, smem, smem, vmem, vmem, smem],
         out_specs=(vmem, vmem),
         scratch_shapes=[
             pltpu.VMEM((dates, 2, rows, cols), jnp.bfloat16),
@@ -340,7 +352,8 @@
             pltpu.VMEM((window, 2, LOOK_ROWS, tiles, looks, LANES), f32),
             pltpu.VMEM((window, looks, LANES), f32),
             pltpu.VMEM((dates * mates, looks, LANES), f32),
-            pltpu.VMEM((dates, mates, looks, looked_cols), f32),
+            pltpu.VMEM((dates, looks, LANES), f32),
+            pltpu.VMEM((image_rows // LOOK_ROWS, LANES), f32),
             pltpu.SemaphoreType.DMA((dates,)),
             pltpu.SemaphoreType.DMA((dates,)),
             pltpu.SemaphoreType.DMA((dates,)),
@@ -348,17 +361,18 @@
             pltpu.SemaphoreType.DMA((3,)),
         ],
         compiler_params=pltpu.CompilerParams(
-            collective_id=0, has_side_effects=True, vmem_limit_bytes=40 * 1024 * 1024
+            collective_id=0, has_side_effects=True, vmem_limit_bytes=62 * 1024 * 1024
         ),
     )(
         full_resolution_frames,
         height_angle_factor,
         normal_spacings,
-        couple_entry_flags,
-        couple_entry_flags,
+        couple_entry_flags.T,
+        couple_entry_flags.T,
         block_target_indices,
         block_target_totals,
     )
+    return jnp.swapaxes(coherence, 2, 3), velocities.T
 
 
 def solution(mesh):

time: 44.3 us -> 42.2 us (0.953)
  the two profiles are of different devices: /device:TPU:27 before, /device:TPU:0 now
where the time goes in v2:
time: 42.2 us; the launch traced here: 42 us
  Pallas kernels  39.3 us (93%)
  local copies, waits for them, and re-layouts  2.03 us (5%)
  between operations  0.65 us (2%)
    pallas_call x1, Pallas kernels, local(): pl.pallas_call(functools.partial(kernel, dates, mates), out_shape=(jax.Sh...  39.3 us
    unnamed x4, local copies, waits for them, and re-layouts  2.03 us

profile of v2, /device:TPU:0, one launch (start us, length us, event | category | flops | bytes accessed | tf_op | source)
XLA Modules:
  0.0 42.0 jit_solution(6555964578555822683)
XLA Ops:
  0.6 39.3 %shard_map.77 = (f32[1,3,32,128]{3,2,1,0:T(8,128)}, f32[15,64]{1,0:T(8,128)}) custom-call(bf16[1,2,512,512]{3,2,1,0:T(8,128)(2,1)} %frames.1, f32[512,512]{1,0:T(8,128)} %heights.1, f32[16]{0:T(128)} %spacings.1, s32[3,16]{1,0:T(4,128)} %bitcast.5, s32[3,16]{1,0:T(4,128)} %bitcast.6, s32[16,64]{1,0:T(8,128)} %targets.1, s32[16]{0:T(128)} %totals.1), custom_call_target="tpu_custom_call" | custom-call | tf_op jit(solution)/shard_map/pallas_call | solution.py:339
  39.9 0.0 copy-start
  39.9 1.4 %copy.10 = f32[1,3,128,32]{2,3,1,0:T(8,128)} copy(f32[1,3,128,32]{2,3,1,0:T(8,128)} %bitcast.3) | data formatting | bytes 98304
  41.4 0.0 copy-done
  41.4 0.6 %copy.11 = f32[64,15]{0,1:T(8,128)} copy(f32[64,15]{0,1:T(8,128)S(1)} %bitcast.4) | data formatting | bytes 7680
Async XLA Ops:
  39.9 1.4 %copy-start = (f32[15,64]{1,0:T(8,128)S(1)}, f32[15,64]{1,0:T(8,128)}, u32[]{:S(2)}) copy-start(f32[15,64]{1,0:T(8,128)} %get-tuple-element.5) | copy-start | bytes 11524

commit v3 on v2

v3 whole, which is shorter than its diff:
```python
import functools

import jax
import jax.numpy as jnp
from jax import lax
from jax.experimental import pallas as pl
from jax.experimental.pallas import tpu as pltpu
from jax.sharding import PartitionSpec as P

LOOK_ROWS = 4
LOOK_COLS = 16
LANES = 128
EPSILON = 1e-06
HIGHEST = lax.Precision.HIGHEST


def iota(shape, axis):
    return lax.broadcasted_iota(jnp.int32, shape, axis)


def sine_cosine(x):
    turns = jnp.round(x * 0.6366197723675814)
    r = (x - turns * 1.5703125) - turns * 4.838267948966e-4
    z = r * r
    s = r + r * z * (-1.6666654611e-1 + z * (8.3321608736e-3 + z * -1.9515295891e-4))
    c = 1.0 - 0.5 * z + z * z * (
        4.166664568298827e-2 + z * (-1.388731625493765e-3 + z * 2.443315711809948e-5)
    )
    quarter = turns.astype(jnp.int32)
    odd = (quarter & 1) == 1
    sine = jnp.where(odd, c, s) * (1 - (quarter & 2)).astype(jnp.float32)
    cosine = jnp.where(odd, s, c) * (1 - ((quarter + 1) & 2)).astype(jnp.float32)
    return sine, cosine


def inverse_map(flags, dates, mates):
    intervals = dates - 1
    rows = -(-intervals // 8) * 8
    pairs = -(-dates * mates // LANES) * LANES
    own_slot = iota((dates, pairs), 1) // mates == iota((dates, pairs), 0)
    spread = jnp.dot(
        flags.astype(jnp.bfloat16),
        jnp.where(own_slot, 1.0, 0.0).astype(jnp.bfloat16),
        preferred_element_type=jnp.float32,
    )
    kind = iota((mates, pairs), 1) % mates == iota((mates, pairs), 0)
    used = jnp.sum(jnp.where(kind, spread, 0.0), axis=0, keepdims=True)
    interval = iota((rows, pairs), 0)
    pair = iota((rows, pairs), 1)
    first = pair // mates
    covered = (interval >= first) & (interval < first + pair % mates + 1) & (interval < intervals)
    right = jnp.where(covered, used, 0.0)
    normal = lax.dot_general(
        right.astype(jnp.bfloat16),
        right.astype(jnp.bfloat16),
        (((1,), (1,)), ((), ())),
        preferred_element_type=jnp.float32,
    )
    down = iota((rows, rows), 0)
    across = iota((rows, rows), 1)
    down_right = iota((rows, pairs), 0)

    def eliminate(t, carry):
        a, b = carry
        row_a = jnp.sum(jnp.where(down == t, a, 0.0), axis=0, keepdims=True)
        row_b = jnp.sum(jnp.where(down_right == t, b, 0.0), axis=0, keepdims=True)
        column = jnp.sum(jnp.where(across == t, a, 0.0), axis=1, keepdims=True)
        pivot = jnp.sum(jnp.where(across[:1] == t, row_a, 0.0), axis=1, keepdims=True)
        row_a = row_a / pivot
        row_b = row_b / pivot
        return (
            jnp.where(down == t, row_a, a - column * row_a),
            jnp.where(down_right == t, row_b, b - column * row_b),
        )

    return lax.fori_loop(0, intervals, eliminate, (normal, right))[1]


def kernel(
    dates,
    mates,
    group,
    frames,
    heights,
    spacings,
    flags_scalar,
    flags_vector,
    targets,
    totals,
    coherence,
    velocities,
    held,
    height_rows,
    natural,
    height_looks,
    rotated,
    powers,
    phases,
    coh,
    gathered,
    gathered_late,
    partial,
    partials,
    send_sem,
    recv_sem,
    coh_send_sem,
    coh_recv_sem,
    late_send_sem,
    late_recv_sem,
    part_send_sem,
    part_recv_sem,
    local_sem,
):
    me = lax.axis_index("tile")
    g = me // group
    q = me % group
    groups = dates // group
    share = dates // group
    half = share // 2
    cols = held.shape[3]
    rows = held.shape[2] // share
    tiles = cols // LANES
    looks = rows // LOOK_ROWS
    looked_cols = cols // LOOK_COLS
    slots = targets.shape[1]
    window = rotated.shape[0]
    base = g * group - mates
    own_slot = q + mates

    def share_rows(member, first, count, unit):
        return pl.ds(pl.multiple_of((member * share + first) * unit, unit), count * unit)

    own_block = pltpu.make_async_copy(
        frames.at[0, :, share_rows(q, 0, share, rows), :], held.at[own_slot], local_sem.at[0]
    )
    own_heights = pltpu.make_async_copy(
        heights.at[share_rows(q, 0, share, rows), :], height_rows, local_sem.at[1]
    )
    own_block.start()
    own_heights.start()
    gathered_late[...] = jnp.zeros_like(gathered_late)

    barrier = pltpu.get_barrier_semaphore()

    def greet(step, carry):
        pl.semaphore_signal(
            barrier,
            inc=1,
            device_id={"tile": (me + step) % dates},
            device_id_type=pl.DeviceIdType.MESH,
        )
        return carry

    lax.fori_loop(1, dates, greet, 0)
    pl.semaphore_wait(barrier, dates - 1)

    def remote(src, dst, send, recv, to):
        return pltpu.make_async_remote_copy(
            src_ref=src,
            dst_ref=dst,
            send_sem=send,
            recv_sem=recv,
            device_id={"tile": to},
            device_id_type=pl.DeviceIdType.MESH,
        )

    def image_copy(member, slot):
        return remote(
            frames.at[0, :, share_rows(member, 0, share, rows), :],
            held.at[slot],
            send_sem.at[1, member],
            recv_sem.at[slot],
            g * group + member,
        )

    def to_previous(member):
        return remote(
            frames.at[0, :, share_rows(member, 0, half, rows), :],
            held.at[q + group + mates, :, pl.ds(0, half * rows), :],
            send_sem.at[0, member],
            recv_sem.at[q + group + mates],
            (g - 1) * group + member,
        )

    def to_next(member):
        return remote(
            frames.at[0, :, share_rows(member, half, share - half, rows), :],
            held.at[q - group + mates, :, pl.ds(half * rows, (share - half) * rows), :],
            send_sem.at[2, member],
            recv_sem.at[q - group + mates],
            (g + 1) * group + member,
        )

    def from_next(slot):
        place = held.at[slot, :, pl.ds(0, half * rows), :]
        return remote(place, place, send_sem.at[0, 0], recv_sem.at[slot], (me + 1) % dates)

    def from_previous(slot):
        place = held.at[slot, :, pl.ds(half * rows, (share - half) * rows), :]
        return remote(place, place, send_sem.at[0, 0], recv_sem.at[slot], (me + 1) % dates)

    feeds_previous = (g > 0) & (q < mates)
    feeds_next = (g < groups - 1) & (q >= group - mates)

    def partner(step):
        return q ^ step if group & (group - 1) == 0 else (q + step) % group

    def send_beyond(member, carry):
        @pl.when(feeds_previous)
        def _():
            to_previous(member).start()

        @pl.when(feeds_next)
        def _():
            to_next(member).start()

        return carry

    def send_image(step, carry):
        image_copy(partner(group - step), own_slot).start()
        return carry

    lax.fori_loop(0, group, send_beyond, 0)
    lax.fori_loop(1, group, send_image, 0)

    rotated[...] = jnp.zeros_like(rotated)
    powers[...] = jnp.zeros_like(powers)
    phases[...] = jnp.zeros_like(phases)
    coh[...] = jnp.zeros_like(coh)
    assert mates * looked_cols <= LANES

    mapping = inverse_map(flags_vector[...], dates, mates)

    look_lane = iota((cols, LANES), 1)
    pooling = jnp.where(
        iota((cols, LANES), 0) // LOOK_COLS == look_lane, 1.0 / (LOOK_ROWS * LOOK_COLS), 0.0
    ).astype(jnp.bfloat16)

    own_block.wait()
    own_heights.wait()

    def one_tile(tile, carry):
        lower = tile // half
        tile_rows = pl.ds(pl.multiple_of(tile * rows, rows), rows)
        tile_looks = pl.ds(pl.multiple_of(tile * looks, looks), looks)
        for c in range(tiles):
            natural[0, c] = height_rows[tile_rows, c * LANES : (c + 1) * LANES]
        for j in range(LOOK_ROWS):
            height_looks[j] = natural[0, :, pl.ds(j, looks, stride=LOOK_ROWS), :]

        def one_date(step, carry):
            slot = step + mates * (1 - lower)
            date = base + slot

            @pl.when((date >= 0) & (date < dates))
            def _():
                visit(step, slot, date)

            return carry

        def visit(step, slot, date):
            @pl.when((tile == 0) & (slot < group + mates) & (slot != own_slot))
            def _():
                image_copy(slot - mates, slot).wait_recv()

            @pl.when((tile == 0) & (slot >= group + mates))
            def _():
                from_next(slot).wait_recv()

            @pl.when((tile == half) & (slot < mates))
            def _():
                from_previous(slot).wait_recv()

            place = slot % window
            for plane in range(2):
                for c in range(tiles):
                    natural[plane, c] = held[
                        slot, plane, tile_rows, c * LANES : (c + 1) * LANES
                    ].astype(jnp.float32)
            spacing = spacings[date]
            power = None
            for j in range(LOOK_ROWS):
                real = natural[0, :, pl.ds(j, looks, stride=LOOK_ROWS), :]
                imag = natural[1, :, pl.ds(j, looks, stride=LOOK_ROWS), :]
                sine, cosine = sine_cosine(spacing * height_looks[j])
                rotated[place, 0, j] = real * cosine + imag * sine
                rotated[place, 1, j] = imag * cosine - real * sine
                energy = real * real + imag * imag
                power = energy if j == 0 else power + energy
            fields = [power]
            for k in range(1, mates + 1):
                other = (slot + window - k) % window
                flat_real = 0.0
                flat_imag = 0.0
                for j in range(LOOK_ROWS):
                    a_real = rotated[other, 0, j]
                    a_imag = rotated[other, 1, j]
                    c_real = rotated[place, 0, j]
                    c_imag = rotated[place, 1, j]
                    flat_real = flat_real + (a_real * c_real + a_imag * c_imag)
                    flat_imag = flat_imag + (a_imag * c_real - a_real * c_imag)
                fields += [flat_real, flat_imag]
            sums = jnp.concatenate(
                [jnp.concatenate([field[c] for c in range(tiles)], axis=1) for field in fields],
                axis=0,
            )
            high = sums.astype(jnp.bfloat16).astype(jnp.float32)
            split = jnp.concatenate([high, sums - high], axis=0).astype(jnp.bfloat16)
            pooled = jnp.dot(split, pooling, preferred_element_type=jnp.float32)
            means = pooled[: sums.shape[0]] + pooled[sums.shape[0] :]
            power_other = means[:looks]
            powers[place] = power_other
            for k in range(1, mates + 1):
                mean_real = means[(2 * k - 1) * looks : 2 * k * looks]
                mean_imag = means[2 * k * looks : (2 * k + 1) * looks]
                power_own = powers[(slot + window - k) % window]
                scale = 1.0 / jnp.sqrt(power_own * power_other + EPSILON)
                amplitude = jnp.sqrt(mean_real * mean_real + mean_imag * mean_imag) * scale

                @pl.when((step >= k) & (date >= k) & (slot >= mates) & (slot - k < group + mates))
                def _():
                    flag = flags_scalar[k - 1, date - k].astype(jnp.float32)
                    shown = amplitude * flag
                    if k > 1:
                        shown = pltpu.roll(shown, (k - 1) * looked_cols, 1)
                    coh[slot - k, tile_looks, :] = coh[slot - k, tile_looks, :] + shown
                    phases[tile, (slot - k) * mates + (k - 1)] = mean_imag * scale

        lax.fori_loop(0, group + mates, one_date, 0)
        return carry

    lax.fori_loop(0, share, one_tile, 0)

    def coh_copy(to, member):
        return remote(
            coh.at[to + mates],
            gathered.at[share_rows(member, 0, share, looks), :],
            coh_send_sem.at[to],
            coh_recv_sem.at[member],
            g * group + to,
        )

    def late_copy(slot, member):
        return remote(
            coh.at[slot, pl.ds(half * looks, (share - half) * looks), :],
            gathered_late.at[share_rows(member, half, share - half, looks), :],
            late_send_sem.at[slot],
            late_recv_sem.at[member],
            (base + slot + dates) % dates,
        )

    own_coh = pltpu.make_async_copy(
        coh.at[own_slot], gathered.at[share_rows(q, 0, share, looks), :], local_sem.at[2]
    )
    own_coh.start()
    lax.fori_loop(
        1, group, lambda step, carry: (coh_copy(partner(group - step), q).start(), carry)[1], 0
    )

    @pl.when(g > 0)
    def _():
        lax.fori_loop(0, mates, lambda slot, carry: (late_copy(slot, q).start(), carry)[1], 0)

    kept = phases.shape[1]
    offset = base * mates
    expand = jnp.where(
        iota((mapping.shape[1], kept * looks), 1) // looks + offset
        == iota((mapping.shape[1], kept * looks), 0),
        1.0,
        0.0,
    )
    wide = jnp.dot(mapping, expand, precision=HIGHEST, preferred_element_type=jnp.float32)

    def part_copy(tile, source, to):
        return remote(
            partial.at[tile],
            partials.at[source],
            part_send_sem.at[tile],
            part_recv_sem.at[source],
            to,
        )

    def own_part(tile):
        return pltpu.make_async_copy(partial.at[tile], partials.at[g], local_sem.at[3])

    def pick(tile, carry):
        whole_tile = q * share + tile
        listed = targets[pl.ds(whole_tile, 1), :]
        diagonal = iota((slots, slots), 0) == iota((slots, slots), 1)
        row_of = (listed // looked_cols).astype(jnp.float32)
        column_of = (listed % looked_cols).astype(jnp.float32)
        row_down = jnp.sum(jnp.where(diagonal, row_of, 0.0), axis=1, keepdims=True)
        column_down = jnp.sum(jnp.where(diagonal, column_of, 0.0), axis=1, keepdims=True)
        by_column = jnp.where(
            iota((slots, LANES), 1).astype(jnp.float32) == column_down, 1.0, 0.0
        )
        flat_phases = phases[tile].reshape(kept * looks, LANES)
        rows_picked = lax.dot_general(
            by_column,
            flat_phases,
            (((1,), (1,)), ((), ())),
            precision=HIGHEST,
            preferred_element_type=jnp.float32,
        )
        lane = iota((slots, kept * looks), 1)
        picked = jnp.where((lane % looks).astype(jnp.float32) == row_down, rows_picked, 0.0)
        result = lax.dot_general(
            wide,
            picked,
            (((1,), (1,)), ((), ())),
            precision=HIGHEST,
            preferred_element_type=jnp.float32,
        )
        partial[tile] = jnp.where(iota(result.shape, 1) < totals[whole_tile], result, 0.0)

        @pl.when(whole_tile == me)
        def _():
            own_part(tile).start()

        @pl.when(whole_tile != me)
        def _():
            part_copy(tile, g, whole_tile).start()

        return carry

    lax.fori_loop(0, share, pick, 0)

    own_coh.wait()

    def finish(step, carry):
        other = (q + step) % group
        image_copy(other, own_slot).wait_send()
        coh_copy(other, q).wait_send()
        coh_copy(other, other).wait_recv()
        return carry

    lax.fori_loop(1, group, finish, 0)

    def finish_beyond(member, carry):
        @pl.when(feeds_previous)
        def _():
            to_previous(member).wait_send()

        @pl.when(feeds_next)
        def _():
            to_next(member).wait_send()
            late_copy(0, member).wait_recv()

        return carry

    lax.fori_loop(0, group, finish_beyond, 0)

    @pl.when(g > 0)
    def _():
        lax.fori_loop(0, mates, lambda slot, carry: (late_copy(slot, q).wait_send(), carry)[1], 0)

    across_rows = jnp.transpose(gathered[...] + gathered_late[...])
    for k in range(mates):
        coherence[0, k] = across_rows[k * looked_cols : (k + 1) * looked_cols]

    def finish_part(tile, carry):
        whole_tile = q * share + tile

        @pl.when(whole_tile == me)
        def _():
            own_part(tile).wait()

        @pl.when(whole_tile != me)
        def _():
            part_copy(tile, g, whole_tile).wait_send()

        return carry

    lax.fori_loop(0, share, finish_part, 0)

    def arrive(source, carry):
        @pl.when(source * group + me // share != me)
        def _():
            part_copy(0, source, (me + 1) % dates).wait_recv()

        return carry

    lax.fori_loop(0, groups, arrive, 0)
    velocities[...] = jnp.sum(partials[...], axis=0)[: dates - 1]


def local(
    full_resolution_frames,
    height_angle_factor,
    normal_spacings,
    couple_entry_flags,
    block_target_indices,
    block_target_totals,
):
    dates, mates = couple_entry_flags.shape
    image_rows, cols = height_angle_factor.shape
    group = 8
    share = dates // group
    assert dates % group == 0 and share % 2 == 0
    rows = image_rows // dates
    tiles = cols // LANES
    looks = rows // LOOK_ROWS
    looked_cols = cols // LOOK_COLS
    slots = block_target_indices.shape[1]
    window = mates + 1
    padded = -(-(dates - 1) // 8) * 8
    f32 = jnp.float32
    vmem = pl.BlockSpec(memory_space=pltpu.VMEM)
    smem = pl.BlockSpec(memory_space=pltpu.SMEM)
    hbm = pl.BlockSpec(memory_space=pltpu.HBM)
    coherence, velocities = pl.pallas_call(
        functools.partial(kernel, dates, mates, group),
        out_shape=(
            jax.ShapeDtypeStruct((1, mates, looked_cols, image_rows // LOOK_ROWS), f32),
            jax.ShapeDtypeStruct((dates - 1, slots), f32),
        ),
        in_specs=[hbm, hbm, smem, smem, vmem, vmem, smem],
        out_specs=(vmem, vmem),
        scratch_shapes=[
            pltpu.VMEM((group + 2 * mates, 2, share * rows, cols), jnp.bfloat16),
            pltpu.VMEM((share * rows, cols), f32),
            pltpu.VMEM((2, tiles, rows, LANES), f32),
            pltpu.VMEM((LOOK_ROWS, tiles, looks, LANES), f32),
            pltpu.VMEM((window, 2, LOOK_ROWS, tiles, looks, LANES), f32),
            pltpu.VMEM((window, looks, LANES), f32),
            pltpu.VMEM((share, (group + mates) * mates, looks, LANES), f32),
            pltpu.VMEM((group + mates, share * looks, LANES), f32),
            pltpu.VMEM((image_rows // LOOK_ROWS, LANES), f32),
            pltpu.VMEM((image_rows // LOOK_ROWS, LANES), f32),
            pltpu.VMEM((share, padded, slots), f32),
            pltpu.VMEM((dates // group, padded, slots), f32),
            pltpu.SemaphoreType.DMA((3, group)),
            pltpu.SemaphoreType.DMA((group + 2 * mates,)),
            pltpu.SemaphoreType.DMA((group,)),
            pltpu.SemaphoreType.DMA((group,)),
            pltpu.SemaphoreType.DMA((mates,)),
            pltpu.SemaphoreType.DMA((group,)),
            pltpu.SemaphoreType.DMA((share,)),
            pltpu.SemaphoreType.DMA((dates // group,)),
            pltpu.SemaphoreType.DMA((4,)),
        ],
        compiler_params=pltpu.CompilerParams(
            collective_id=0, has_side_effects=True, vmem_limit_bytes=62 * 1024 * 1024
        ),
    )(
        full_resolution_frames,
        height_angle_factor,
        normal_spacings,
        couple_entry_flags.T,
        couple_entry_flags.T,
        block_target_indices,
        block_target_totals,
    )
    return jnp.swapaxes(coherence, 2, 3), velocities.T


def solution(mesh):
    in_specs = (
        P(("grp", "tile"), None, None, None),
        P("grp", None),
        P("grp"),
        P(),
        P("grp", None),
        P("grp"),
    )
    out_specs = (P(("grp", "tile"), None, None, None), P(("grp", "tile"), None))
    return jax.shard_map(local, mesh=mesh, in_specs=in_specs, out_specs=out_specs, check_vma=False)
```

time: 42.2 us -> 39.7 us (0.941)
  the two profiles are of different devices: /device:TPU:0 before, /device:TPU:1 now
where the time goes in v3:
time: 39.7 us; the launch traced here: 39.4 us
  Pallas kernels  36.7 us (92%)
  local copies, waits for them, and re-layouts  2.03 us (5%)
  between operations  0.65 us (2%)
    pallas_call x1, Pallas kernels, local(): pl.pallas_call(functools.partial(kernel, dates, mates, group), out_shape=...  36.7 us
    unnamed x4, local copies, waits for them, and re-layouts  2.03 us

profile of v3, /device:TPU:1, one launch (start us, length us, event | category | flops | bytes accessed | tf_op | source)
XLA Modules:
  0.0 39.4 jit_solution(5027471066114349928)
XLA Ops:
  0.6 36.7 %shard_map.77 = (f32[1,3,32,128]{3,2,1,0:T(8,128)}, f32[15,64]{1,0:T(8,128)}) custom-call(bf16[1,2,512,512]{3,2,1,0:T(8,128)(2,1)} %frames.1, f32[512,512]{1,0:T(8,128)} %heights.1, f32[16]{0:T(128)} %spacings.1, s32[3,16]{1,0:T(4,128)} %bitcast.5, s32[3,16]{1,0:T(4,128)} %bitcast.6, s32[16,64]{1,0:T(8,128)} %targets.1, s32[16]{0:T(128)} %totals.1), custom_call_target="tpu_custom_call" | custom-call | tf_op jit(solution)/shard_map/pallas_call | solution.py:511
  37.4 0.0 copy-start
  37.4 1.4 %copy.10 = f32[1,3,128,32]{2,3,1,0:T(8,128)} copy(f32[1,3,128,32]{2,3,1,0:T(8,128)} %bitcast.3) | data formatting | bytes 98304
  38.8 0.0 copy-done
  38.8 0.6 %copy.11 = f32[64,15]{0,1:T(8,128)} copy(f32[64,15]{0,1:T(8,128)S(1)} %bitcast.4) | data formatting | bytes 7680
Async XLA Ops:
  37.4 1.4 %copy-start = (f32[15,64]{1,0:T(8,128)S(1)}, f32[15,64]{1,0:T(8,128)}, u32[]{:S(2)}) copy-start(f32[15,64]{1,0:T(8,128)} %get-tuple-element.5) | copy-start | bytes 11524

commit v4 on v3

--- a/solution.py
+++ b/solution.py
@@ -164,12 +164,12 @@
             device_id_type=pl.DeviceIdType.MESH,
         )
 
-    def image_copy(member, slot):
+    def image_copy(member, slot, part):
         return remote(
-            frames.at[0, :, share_rows(member, 0, share, rows), :],
-            held.at[slot],
-            send_sem.at[1, member],
-            recv_sem.at[slot],
+            frames.at[0, :, share_rows(member, part * half, half, rows), :],
+            held.at[slot, :, pl.ds(part * half * rows, half * rows), :],
+            send_sem.at[1 + part, member],
+            recv_sem.at[part, slot],
             g * group + member,
         )
 
@@ -178,7 +178,7 @@
             frames.at[0, :, share_rows(member, 0, half, rows), :],
             held.at[q + group + mates, :, pl.ds(0, half * rows), :],
             send_sem.at[0, member],
-            recv_sem.at[q + group + mates],
+            recv_sem.at[0, q + group + mates],
             (g - 1) * group + member,
         )
 
@@ -186,18 +186,14 @@
         return remote(
             frames.at[0, :, share_rows(member, half, share - half, rows), :],
             held.at[q - group + mates, :, pl.ds(half * rows, (share - half) * rows), :],
-            send_sem.at[2, member],
-            recv_sem.at[q - group + mates],
+            send_sem.at[3, member],
+            recv_sem.at[1, q - group + mates],
             (g + 1) * group + member,
         )
 
-    def from_next(slot):
-        place = held.at[slot, :, pl.ds(0, half * rows), :]
-        return remote(place, place, send_sem.at[0, 0], recv_sem.at[slot], (me + 1) % dates)
-
-    def from_previous(slot):
-        place = held.at[slot, :, pl.ds(half * rows, (share - half) * rows), :]
-        return remote(place, place, send_sem.at[0, 0], recv_sem.at[slot], (me + 1) % dates)
+    def arrival(slot, part):
+        place = held.at[slot, :, pl.ds(part * half * rows, half * rows), :]
+        return remote(place, place, send_sem.at[0, 0], recv_sem.at[part, slot], (me + 1) % dates)
 
     feeds_previous = (g > 0) & (q < mates)
     feeds_next = (g < groups - 1) & (q >= group - mates)
@@ -205,23 +201,27 @@
     def partner(step):
         return q ^ step if group & (group - 1) == 0 else (q + step) % group
 
-    def send_beyond(member, carry):
-        @pl.when(feeds_previous)
-        def _():
-            to_previous(member).start()
-
-        @pl.when(feeds_next)
-        def _():
-            to_next(member).start()
-
-        return carry
-
-    def send_image(step, carry):
-        image_copy(partner(group - step), own_slot).start()
-        return carry
-
-    lax.fori_loop(0, group, send_beyond, 0)
-    lax.fori_loop(1, group, send_image, 0)
+    @pl.when(feeds_previous)
+    def _():
+        lax.fori_loop(0, group, lambda member, carry: (to_previous(member).start(), carry)[1], 0)
+
+    lax.fori_loop(
+        1,
+        group,
+        lambda step, carry: (image_copy(partner(group - step), own_slot, 0).start(), carry)[1],
+        0,
+    )
+
+    @pl.when(feeds_next)
+    def _():
+        lax.fori_loop(0, group, lambda member, carry: (to_next(member).start(), carry)[1], 0)
+
+    lax.fori_loop(
+        1,
+        group,
+        lambda step, carry: (image_copy(partner(group - step), own_slot, 1).start(), carry)[1],
+        0,
+    )
 
     rotated[...] = jnp.zeros_like(rotated)
     powers[...] = jnp.zeros_like(powers)
@@ -235,6 +235,66 @@
     pooling = jnp.where(
         iota((cols, LANES), 0) // LOOK_COLS == look_lane, 1.0 / (LOOK_ROWS * LOOK_COLS), 0.0
     ).astype(jnp.bfloat16)
+
+    kept = phases.shape[1]
+    offset = base * mates
+    expand = jnp.where(
+        iota((mapping.shape[1], kept * looks), 1) // looks + offset
+        == iota((mapping.shape[1], kept * looks), 0),
+        1.0,
+        0.0,
+    )
+    wide = jnp.dot(mapping, expand, precision=HIGHEST, preferred_element_type=jnp.float32)
+
+    def part_copy(tile, source, to):
+        return remote(
+            partial.at[tile],
+            partials.at[source],
+            part_send_sem.at[tile],
+            part_recv_sem.at[source],
+            to,
+        )
+
+    def own_part(tile):
+        return pltpu.make_async_copy(partial.at[tile], partials.at[g], local_sem.at[3])
+
+    def pick(tile):
+        whole_tile = q * share + tile
+        listed = targets[pl.ds(whole_tile, 1), :]
+        diagonal = iota((slots, slots), 0) == iota((slots, slots), 1)
+        row_of = (listed // looked_cols).astype(jnp.float32)
+        column_of = (listed % looked_cols).astype(jnp.float32)
+        row_down = jnp.sum(jnp.where(diagonal, row_of, 0.0), axis=1, keepdims=True)
+        column_down = jnp.sum(jnp.where(diagonal, column_of, 0.0), axis=1, keepdims=True)
+        by_column = jnp.where(
+            iota((slots, LANES), 1).astype(jnp.float32) == column_down, 1.0, 0.0
+        )
+        flat_phases = phases[tile].reshape(kept * looks, LANES)
+        rows_picked = lax.dot_general(
+            by_column,
+            flat_phases,
+            (((1,), (1,)), ((), ())),
+            precision=HIGHEST,
+            preferred_element_type=jnp.float32,
+        )
+        lane = iota((slots, kept * looks), 1)
+        picked = jnp.where((lane % looks).astype(jnp.float32) == row_down, rows_picked, 0.0)
+        result = lax.dot_general(
+            wide,
+            picked,
+            (((1,), (1,)), ((), ())),
+            precision=HIGHEST,
+            preferred_element_type=jnp.float32,
+        )
+        partial[tile] = jnp.where(iota(result.shape, 1) < totals[whole_tile], result, 0.0)
+
+        @pl.when(whole_tile == me)
+        def _():
+            own_part(tile).start()
+
+        @pl.when(whole_tile != me)
+        def _():
+            part_copy(tile, g, whole_tile).start()
 
     own_block.wait()
     own_heights.wait()
@@ -259,17 +319,13 @@
             return carry
 
         def visit(step, slot, date):
-            @pl.when((tile == 0) & (slot < group + mates) & (slot != own_slot))
+            @pl.when((tile == 0) & (slot != own_slot))
             def _():
-                image_copy(slot - mates, slot).wait_recv()
-
-            @pl.when((tile == 0) & (slot >= group + mates))
+                arrival(slot, 0).wait_recv()
+
+            @pl.when((tile == half) & (slot != own_slot))
             def _():
-                from_next(slot).wait_recv()
-
-            @pl.when((tile == half) & (slot < mates))
-            def _():
-                from_previous(slot).wait_recv()
+                arrival(slot, 1).wait_recv()
 
             place = slot % window
             for plane in range(2):
@@ -327,6 +383,11 @@
                     phases[tile, (slot - k) * mates + (k - 1)] = mean_imag * scale
 
         lax.fori_loop(0, group + mates, one_date, 0)
+
+        @pl.when(tile < share - 1)
+        def _():
+            pick(tile)
+
         return carry
 
     lax.fori_loop(0, share, one_tile, 0)
@@ -361,75 +422,14 @@
     def _():
         lax.fori_loop(0, mates, lambda slot, carry: (late_copy(slot, q).start(), carry)[1], 0)
 
-    kept = phases.shape[1]
-    offset = base * mates
-    expand = jnp.where(
-        iota((mapping.shape[1], kept * looks), 1) // looks + offset
-        == iota((mapping.shape[1], kept * looks), 0),
-        1.0,
-        0.0,
-    )
-    wide = jnp.dot(mapping, expand, precision=HIGHEST, preferred_element_type=jnp.float32)
-
-    def part_copy(tile, source, to):
-        return remote(
-            partial.at[tile],
-            partials.at[source],
-            part_send_sem.at[tile],
-            part_recv_sem.at[source],
-            to,
-        )
-
-    def own_part(tile):
-        return pltpu.make_async_copy(partial.at[tile], partials.at[g], local_sem.at[3])
-
-    def pick(tile, carry):
-        whole_tile = q * share + tile
-        listed = targets[pl.ds(whole_tile, 1), :]
-        diagonal = iota((slots, slots), 0) == iota((slots, slots), 1)
-        row_of = (listed // looked_cols).astype(jnp.float32)
-        column_of = (listed % looked_cols).astype(jnp.float32)
-        row_down = jnp.sum(jnp.where(diagonal, row_of, 0.0), axis=1, keepdims=True)
-        column_down = jnp.sum(jnp.where(diagonal, column_of, 0.0), axis=1, keepdims=True)
-        by_column = jnp.where(
-            iota((slots, LANES), 1).astype(jnp.float32) == column_down, 1.0, 0.0
-        )
-        flat_phases = phases[tile].reshape(kept * looks, LANES)
-        rows_picked = lax.dot_general(
-            by_column,
-            flat_phases,
-            (((1,), (1,)), ((), ())),
-            precision=HIGHEST,
-            preferred_element_type=jnp.float32,
-        )
-        lane = iota((slots, kept * looks), 1)
-        picked = jnp.where((lane % looks).astype(jnp.float32) == row_down, rows_picked, 0.0)
-        result = lax.dot_general(
-            wide,
-            picked,
-            (((1,), (1,)), ((), ())),
-            precision=HIGHEST,
-            preferred_element_type=jnp.float32,
-        )
-        partial[tile] = jnp.where(iota(result.shape, 1) < totals[whole_tile], result, 0.0)
-
-        @pl.when(whole_tile == me)
-        def _():
-            own_part(tile).start()
-
-        @pl.when(whole_tile != me)
-        def _():
-            part_copy(tile, g, whole_tile).start()
-
-        return carry
-
-    lax.fori_loop(0, share, pick, 0)
+    pick(share - 1)
 
     own_coh.wait()
 
     def finish(step, carry):
         other = (q + step) % group
-        image_copy(other, own_slot).wait_send()
+        image_copy(other, own_slot, 0).wait_send()
+        image_copy(other, own_slot, 1).wait_send()
         coh_copy(other, q).wait_send()
         coh_copy(other, other).wait_recv()
         return carry
@@ -529,8 +529,8 @@
             pltpu.VMEM((image_rows // LOOK_ROWS, LANES), f32),
             pltpu.VMEM((share, padded, slots), f32),
             pltpu.VMEM((dates // group, padded, slots), f32),
-            pltpu.SemaphoreType.DMA((3, group)),
-            pltpu.SemaphoreType.DMA((group + 2 * mates,)),
+            pltpu.SemaphoreType.DMA((4, group)),
+            pltpu.SemaphoreType.DMA((2, group + 2 * mates)),
             pltpu.SemaphoreType.DMA((group,)),
             pltpu.SemaphoreType.DMA((group,)),
             pltpu.SemaphoreType.DMA((mates,)),

time: 39.7 us -> 35.6 us (0.90)
  Pallas kernels: 36.7 us -> 32.7 us
    pallas_call x1, Pallas kernels: 36.7 us -> 32.7 us  [local(): pl.pallas_call(functools.partial(kernel, dates, mates, group), out_shape=...]
where the time goes in v4:
time: 35.6 us; the launch traced here: 35.4 us
  Pallas kernels  32.7 us (92%)
  local copies, waits for them, and re-layouts  2.03 us (6%)
  between operations  0.65 us (2%)
    pallas_call x1, Pallas kernels, local(): pl.pallas_call(functools.partial(kernel, dates, mates, group), out_shape=...  32.7 us
    unnamed x4, local copies, waits for them, and re-layouts  2.03 us

profile of v4, /device:TPU:1, one launch (start us, length us, event | category | flops | bytes accessed | tf_op | source)
XLA Modules:
  0.0 35.4 jit_solution(13006353600279887670)
XLA Ops:
  0.6 32.7 %shard_map.77 = (f32[1,3,32,128]{3,2,1,0:T(8,128)}, f32[15,64]{1,0:T(8,128)}) custom-call(bf16[1,2,512,512]{3,2,1,0:T(8,128)(2,1)} %frames.1, f32[512,512]{1,0:T(8,128)} %heights.1, f32[16]{0:T(128)} %spacings.1, s32[3,16]{1,0:T(4,128)} %bitcast.5, s32[3,16]{1,0:T(4,128)} %bitcast.6, s32[16,64]{1,0:T(8,128)} %targets.1, s32[16]{0:T(128)} %totals.1), custom_call_target="tpu_custom_call" | custom-call | tf_op jit(solution)/shard_map/pallas_call | solution.py:511
  33.3 0.0 copy-start
  33.3 1.4 %copy.10 = f32[1,3,128,32]{2,3,1,0:T(8,128)} copy(f32[1,3,128,32]{2,3,1,0:T(8,128)} %bitcast.3) | data formatting | bytes 98304
  34.8 0.0 copy-done
  34.8 0.6 %copy.11 = f32[64,15]{0,1:T(8,128)} copy(f32[64,15]{0,1:T(8,128)S(1)} %bitcast.4) | data formatting | bytes 7680
Async XLA Ops:
  33.3 1.4 %copy-start = (f32[15,64]{1,0:T(8,128)S(1)}, f32[15,64]{1,0:T(8,128)}, u32[]{:S(2)}) copy-start(f32[15,64]{1,0:T(8,128)} %get-tuple-element.5) | copy-start | bytes 11524

commit v5 on v4

--- a/solution.py
+++ b/solution.py
@@ -312,40 +312,28 @@
             slot = step + mates * (1 - lower)
             date = base + slot
 
-            @pl.when((date >= 0) & (date < dates))
+            @pl.when((date >= 0) & (date <= dates))
             def _():
                 visit(step, slot, date)
 
             return carry
 
         def visit(step, slot, date):
-            @pl.when((tile == 0) & (slot != own_slot))
+            real_date = (step < group + mates) & (date < dates)
+
+            @pl.when(real_date & (tile == 0) & (slot != own_slot))
             def _():
                 arrival(slot, 0).wait_recv()
 
-            @pl.when((tile == half) & (slot != own_slot))
+            @pl.when(real_date & (tile == half) & (slot != own_slot))
             def _():
                 arrival(slot, 1).wait_recv()
 
-            place = slot % window
-            for plane in range(2):
-                for c in range(tiles):
-                    natural[plane, c] = held[
-                        slot, plane, tile_rows, c * LANES : (c + 1) * LANES
-                    ].astype(jnp.float32)
-            spacing = spacings[date]
-            power = None
-            for j in range(LOOK_ROWS):
-                real = natural[0, :, pl.ds(j, looks, stride=LOOK_ROWS), :]
-                imag = natural[1, :, pl.ds(j, looks, stride=LOOK_ROWS), :]
-                sine, cosine = sine_cosine(spacing * height_looks[j])
-                rotated[place, 0, j] = real * cosine + imag * sine
-                rotated[place, 1, j] = imag * cosine - real * sine
-                energy = real * real + imag * imag
-                power = energy if j == 0 else power + energy
-            fields = [power]
+            before = slot + window - 1
+            place = before % window
+            fields = []
             for k in range(1, mates + 1):
-                other = (slot + window - k) % window
+                other = (before + window - k) % window
                 flat_real = 0.0
                 flat_imag = 0.0
                 for j in range(LOOK_ROWS):
@@ -356,6 +344,22 @@
                     flat_real = flat_real + (a_real * c_real + a_imag * c_imag)
                     flat_imag = flat_imag + (a_imag * c_real - a_real * c_imag)
                 fields += [flat_real, flat_imag]
+            for plane in range(2):
+                for c in range(tiles):
+                    natural[plane, c] = held[
+                        slot - step // (group + mates), plane, tile_rows, c * LANES : (c + 1) * LANES
+                    ].astype(jnp.float32)
+            spacing = spacings[date - date // dates]
+            power = None
+            for j in range(LOOK_ROWS):
+                real = natural[0, :, pl.ds(j, looks, stride=LOOK_ROWS), :]
+                imag = natural[1, :, pl.ds(j, looks, stride=LOOK_ROWS), :]
+                sine, cosine = sine_cosine(spacing * height_looks[j])
+                rotated[slot % window, 0, j] = real * cosine + imag * sine
+                rotated[slot % window, 1, j] = imag * cosine - real * sine
+                energy = real * real + imag * imag
+                power = energy if j == 0 else power + energy
+            fields = [power] + fields
             sums = jnp.concatenate(
                 [jnp.concatenate([field[c] for c in range(tiles)], axis=1) for field in fields],
                 axis=0,
@@ -364,25 +368,27 @@
             split = jnp.concatenate([high, sums - high], axis=0).astype(jnp.bfloat16)
             pooled = jnp.dot(split, pooling, preferred_element_type=jnp.float32)
             means = pooled[: sums.shape[0]] + pooled[sums.shape[0] :]
-            power_other = means[:looks]
-            powers[place] = power_other
+            power_other = powers[place]
+            power_next = means[:looks]
             for k in range(1, mates + 1):
                 mean_real = means[(2 * k - 1) * looks : 2 * k * looks]
                 mean_imag = means[2 * k * looks : (2 * k + 1) * looks]
-                power_own = powers[(slot + window - k) % window]
+                power_own = powers[(before + window - k) % window]
                 scale = 1.0 / jnp.sqrt(power_own * power_other + EPSILON)
                 amplitude = jnp.sqrt(mean_real * mean_real + mean_imag * mean_imag) * scale
 
-                @pl.when((step >= k) & (date >= k) & (slot >= mates) & (slot - k < group + mates))
+                @pl.when((step > k) & (date > k) & (slot > mates) & (slot - k <= group + mates))
                 def _():
-                    flag = flags_scalar[k - 1, date - k].astype(jnp.float32)
+                    flag = flags_scalar[k - 1, date - 1 - k].astype(jnp.float32)
                     shown = amplitude * flag
                     if k > 1:
                         shown = pltpu.roll(shown, (k - 1) * looked_cols, 1)
-                    coh[slot - k, tile_looks, :] = coh[slot - k, tile_looks, :] + shown
-                    phases[tile, (slot - k) * mates + (k - 1)] = mean_imag * scale
-
-        lax.fori_loop(0, group + mates, one_date, 0)
+                    coh[slot - 1 - k, tile_looks, :] = coh[slot - 1 - k, tile_looks, :] + shown
+                    phases[tile, (slot - 1 - k) * mates + (k - 1)] = mean_imag * scale
+
+            powers[slot % window] = power_next
+
+        lax.fori_loop(0, group + mates + 1, one_date, 0)
 
         @pl.when(tile < share - 1)
         def _():
@@ -502,7 +508,7 @@
     looks = rows // LOOK_ROWS
     looked_cols = cols // LOOK_COLS
     slots = block_target_indices.shape[1]
-    window = mates + 1
+    window = mates + 2
     padded = -(-(dates - 1) // 8) * 8
     f32 = jnp.float32
     vmem = pl.BlockSpec(memory_space=pltpu.VMEM)

time: 35.6 us -> 36.5 us (1.025)
  Pallas kernels: 32.7 us -> 33.6 us
    pallas_call x1, Pallas kernels: 32.7 us -> 33.6 us  [local(): pl.pallas_call(functools.partial(kernel, dates, mates, group), out_shape=...]
where the time goes in v5:
time: 36.5 us; the launch traced here: 36.2 us
  Pallas kernels  33.6 us (92%)
  local copies, waits for them, and re-layouts  2.03 us (6%)
  between operations  0.65 us (2%)
    pallas_call x1, Pallas kernels, local(): pl.pallas_call(functools.partial(kernel, dates, mates, group), out_shape=...  33.6 us
    unnamed x4, local copies, waits for them, and re-layouts  2.03 us

profile of v5, /device:TPU:1, one launch (start us, length us, event | category | flops | bytes accessed | tf_op | source)
XLA Modules:
  0.0 36.2 jit_solution(12116875066889000424)
XLA Ops:
  0.6 33.6 %shard_map.77 = (f32[1,3,32,128]{3,2,1,0:T(8,128)}, f32[15,64]{1,0:T(8,128)}) custom-call(bf16[1,2,512,512]{3,2,1,0:T(8,128)(2,1)} %frames.1, f32[512,512]{1,0:T(8,128)} %heights.1, f32[16]{0:T(128)} %spacings.1, s32[3,16]{1,0:T(4,128)} %bitcast.5, s32[3,16]{1,0:T(4,128)} %bitcast.6, s32[16,64]{1,0:T(8,128)} %targets.1, s32[16]{0:T(128)} %totals.1), custom_call_target="tpu_custom_call" | custom-call | tf_op jit(solution)/shard_map/pallas_call | solution.py:517
  34.2 0.0 copy-start
  34.2 1.4 %copy.10 = f32[1,3,128,32]{2,3,1,0:T(8,128)} copy(f32[1,3,128,32]{2,3,1,0:T(8,128)} %bitcast.3) | data formatting | bytes 98304
  35.6 0.0 copy-done
  35.6 0.6 %copy.11 = f32[64,15]{0,1:T(8,128)} copy(f32[64,15]{0,1:T(8,128)S(1)} %bitcast.4) | data formatting | bytes 7680
Async XLA Ops:
  34.2 1.4 %copy-start = (f32[15,64]{1,0:T(8,128)S(1)}, f32[15,64]{1,0:T(8,128)}, u32[]{:S(2)}) copy-start(f32[15,64]{1,0:T(8,128)} %get-tuple-element.5) | copy-start | bytes 11524

commit v6 on v4

--- a/solution.py
+++ b/solution.py
@@ -370,7 +370,7 @@
                 mean_real = means[(2 * k - 1) * looks : 2 * k * looks]
                 mean_imag = means[2 * k * looks : (2 * k + 1) * looks]
                 power_own = powers[(slot + window - k) % window]
-                scale = 1.0 / jnp.sqrt(power_own * power_other + EPSILON)
+                scale = lax.rsqrt(power_own * power_other + EPSILON)
                 amplitude = jnp.sqrt(mean_real * mean_real + mean_imag * mean_imag) * scale
 
                 @pl.when((step >= k) & (date >= k) & (slot >= mates) & (slot - k < group + mates))

time: 35.6 us -> 35.3 us (level)
  no operation moved by 1% of the time
where the time goes in v6:
time: 35.3 us; the launch traced here: 35 us
  Pallas kernels  32.4 us (92%)
  local copies, waits for them, and re-layouts  2.03 us (6%)
  between operations  0.65 us (2%)
    pallas_call x1, Pallas kernels, local(): pl.pallas_call(functools.partial(kernel, dates, mates, group), out_shape=...  32.4 us
    unnamed x4, local copies, waits for them, and re-layouts  2.03 us

profile of v6, /device:TPU:1, one launch (start us, length us, event | category | flops | bytes accessed | tf_op | source)
XLA Modules:
  0.0 35.0 jit_solution(15334330269272169117)
XLA Ops:
  0.6 32.4 %shard_map.77 = (f32[1,3,32,128]{3,2,1,0:T(8,128)}, f32[15,64]{1,0:T(8,128)}) custom-call(bf16[1,2,512,512]{3,2,1,0:T(8,128)(2,1)} %frames.1, f32[512,512]{1,0:T(8,128)} %heights.1, f32[16]{0:T(128)} %spacings.1, s32[3,16]{1,0:T(4,128)} %bitcast.5, s32[3,16]{1,0:T(4,128)} %bitcast.6, s32[16,64]{1,0:T(8,128)} %targets.1, s32[16]{0:T(128)} %totals.1), custom_call_target="tpu_custom_call" | custom-call | tf_op jit(solution)/shard_map/pallas_call | solution.py:511
  33.0 0.0 copy-start
  33.0 1.4 %copy.10 = f32[1,3,128,32]{2,3,1,0:T(8,128)} copy(f32[1,3,128,32]{2,3,1,0:T(8,128)} %bitcast.3) | data formatting | bytes 98304
  34.4 0.0 copy-done
  34.4 0.6 %copy.11 = f32[64,15]{0,1:T(8,128)} copy(f32[64,15]{0,1:T(8,128)S(1)} %bitcast.4) | data formatting | bytes 7680
Async XLA Ops:
  33.0 1.4 %copy-start = (f32[15,64]{1,0:T(8,128)S(1)}, f32[15,64]{1,0:T(8,128)}, u32[]{:S(2)}) copy-start(f32[15,64]{1,0:T(8,128)} %get-tuple-element.5) | copy-start | bytes 11524
